TPU v7x, 128 devices: a whole 4x4x4 slice. The times are simulated.
128 devices in a mesh: dp: 16 (over x, z), expert: 8 (over y, core).
Axes of the slice: x: 4, y: 4, z: 4, core: 2. Of those that a mesh axis runs over, the one named last changes fastest.
Arguments:
- tokens: bfloat16 [4096, 8192], P('dp', 'expert'), may hold values from -6 to 6
- w_in: bfloat16 [8192, 32768], P('expert', 'dp'), may hold values from -0.0625 to 0.0625
- w_out: bfloat16 [32768, 8192], P('dp', 'expert'), may hold values from -0.03125 to 0.03125
- chosen: int32 [16, 64], P('dp'), may hold values from 0 to 255, as said below
- counts: int32 [16], P('dp'), may hold values from 1 to 64, 512 in all
- gates: float32 [16, 64], P('dp'), may hold values from 0.1 to 1
- cotangent: bfloat16 [4096, 8192], P('dp', 'expert'), may hold values from -6 to 6
Outputs:
- mixed: bfloat16 [4096, 8192], P('dp', 'expert')
- d_tokens: bfloat16 [4096, 8192], P('dp', 'expert')
- d_w_in: bfloat16 [8192, 32768], P('expert', 'dp')
- d_w_out: bfloat16 [32768, 8192], P('dp', 'expert')
Inputs may be any that keep to these rules, and one draw needn't show every extreme that they name: `chosen`: row i lists local indices of tokens of shard i; its first counts[i] entries name the tokens the expert chose there and are distinct; the other entries are ignored. `counts`: entry i is the number of used entries of row i of chosen; the entries sum to exactly 512, and some shard has exactly 64.
All inputs are finite; a program needn't handle non-finite values.
Results may differ from a plain program's by a relative error of at most 0.029.
Values may be sent and summed in bfloat16 or wider, within the bound.
A program may use at most 128 MiB of HBM per device.

v0:
```python
import jax
import jax.numpy as jnp
from jax import lax
from jax.sharding import PartitionSpec as P

half_root = 0.7071067811865476
inv_root_tau = 0.3989422804014327


def gelu_pair(pre_act):
    cdf_part = 0.5 * (1.0 + lax.erf(pre_act * half_root))
    slopes = cdf_part + pre_act * jnp.exp(-0.5 * pre_act * pre_act) * inv_root_tau
    return (pre_act * cdf_part, slopes)


def hidden_rows(part_rows, finish):
    summed = lax.psum(part_rows, "expert").astype(jnp.float32)
    return finish(summed)


def contract_rows(left_side, right_side, flip_axis):
    return lax.dot_general(
        left_side, right_side, (((1,), (flip_axis,)), ((), ())), preferred_element_type=jnp.float32
    )


def local(tokens, w_in, w_out, chosen, counts, gates, cotangent):
    slot_count = chosen.shape[1]
    tok_rows = tokens.shape[0]
    feat_width = tokens.shape[1]
    places = chosen[0]
    live_mask = jnp.arange(slot_count) < counts[0]
    weight_rows = jnp.where(live_mask, gates[0], 0.0)
    picked = jnp.where(live_mask[:, None], tokens[places], jnp.zeros((), jnp.bfloat16))
    grad_pick = (weight_rows[:, None] * cotangent[places].astype(jnp.float32)).astype(jnp.bfloat16)

    def forward_finish(pre_act):
        activated, slopes = gelu_pair(pre_act)
        return (activated.astype(jnp.bfloat16), slopes)

    piece_rows = lax.all_gather(picked, "dp", axis=0, tiled=True)
    pre_part = jnp.dot(piece_rows, w_in, preferred_element_type=jnp.float32).astype(jnp.bfloat16)

    def send_home(left_side, right_side, flip_axis):
        return lax.psum_scatter(
            contract_rows(left_side, right_side, flip_axis).astype(jnp.bfloat16),
            "dp",
            scatter_dimension=0,
            tiled=True,
        ).astype(jnp.float32)

    hidden, slopes = hidden_rows(pre_part, forward_finish)
    expert_rows = send_home(hidden, w_out, 0)
    mixed_rows = jnp.where(live_mask[:, None], weight_rows[:, None] * expert_rows, 0.0)
    mixed = (
        jnp.zeros((tok_rows, feat_width), jnp.float32)
        .at[places]
        .add(mixed_rows)
        .astype(jnp.bfloat16)
    )
    back_piece_rows = lax.all_gather(grad_pick, "dp", axis=0, tiled=True)
    back_part = contract_rows(back_piece_rows, w_out, 1).astype(jnp.bfloat16)

    def backward_finish(back_hidden):
        return ((back_hidden * slopes).astype(jnp.bfloat16), slopes)

    back_pre, unused_slopes = hidden_rows(back_part, backward_finish)
    d_w_out = lax.dot_general(
        hidden, back_piece_rows, (((0,), (0,)), ((), ())), preferred_element_type=jnp.float32
    ).astype(jnp.bfloat16)
    d_w_in = lax.dot_general(
        piece_rows, back_pre, (((0,), (0,)), ((), ())), preferred_element_type=jnp.float32
    ).astype(jnp.bfloat16)
    d_rows = send_home(back_pre, w_in, 1)
    d_rows = jnp.where(live_mask[:, None], d_rows, 0.0)
    d_tokens = (
        jnp.zeros((tok_rows, feat_width), jnp.float32).at[places].add(d_rows).astype(jnp.bfloat16)
    )
    return (mixed, d_tokens, d_w_in, d_w_out)


def solution(mesh):
    in_specs = (
        P("dp", "expert"),
        P("expert", "dp"),
        P("dp", "expert"),
        P("dp", None),
        P("dp"),
        P("dp", None),
        P("dp", "expert"),
    )
    out_specs = (P("dp", "expert"), P("dp", "expert"), P("expert", "dp"), P("dp", "expert"))
    return jax.shard_map(local, mesh=mesh, in_specs=in_specs, out_specs=out_specs, check_vma=False)
```

profile of v0, /device:TPU:0, one launch (start us, length us, event | category | flops | bytes accessed | tf_op | source)
XLA Modules:
  0.0 396.5 jit_solution(9167018944662495016)
XLA Ops:
  7.2 0.0 copy-start
  7.2 0.0 all-gather.3.cloned.1.call-start
  7.9 0.7 fusion.23
  8.6 0.0 copy-done
  8.6 0.7 gather_fusion
  9.3 0.7 broadcast_select_fusion
  10.1 0.0 all-gather.3.cloned.1.call-update
  10.1 0.0 all-gather.5.cloned.1.call-start
  10.1 1.9 gather_fusion.1
  12.0 0.7 bitcast_select_fusion
  12.7 0.7 multiply_convert_fusion
  13.4 0.0 all-gather.5.cloned.1.call-update
  13.5 0.0 all-reduce.3.cloned.1.call-start
  13.5 45.0 %all-gather.3.cloned.1.call-done = bf16[1024,1024]{1,0:T(8,128)(2,1)} async-done(((bf16[64,1024]{1,0:T(8,128)(2,1)}), bf16[1024,1024]{1,0:T(8,128)(2,1)}) %all-gather.3.cloned.1.call-update) | async-done | bytes 2097168 | tf_op jit(solution)/shard_map/all_gather | solution.py:41
  58.5 9.3 %convolution_convert_fusion.3 = bf16[1024,2048]{1,0:T(8,128)(2,1)} fusion(bf16[1024,1024]{1,0:T(8,128)(2,1)} %all-gather.3.cloned.1.call-done, bf16[1024,2048]{1,0:T(8,128)(2,1)} %param.8), kind=kOutput, calls=%fused_computation.21 | convolution fusion | flops 4297064448 | bytes 10485760 | tf_op jit(solution)/shard_map/dot_general | solution.py:42
  67.8 37.9 %all-gather.5.cloned.1.call-done = bf16[1024,1024]{1,0:T(8,128)(2,1)} async-done(((bf16[64,1024]{1,0:T(8,128)(2,1)}), bf16[1024,1024]{1,0:T(8,128)(2,1)}) %all-gather.5.cloned.1.call-update) | async-done | bytes 2097168 | tf_op jit(solution)/shard_map/all_gather | solution.py:61
  105.8 9.4 %convolution_convert_fusion.2 = bf16[1024,2048]{1,0:T(8,128)(2,1)} fusion(bf16[1024,1024]{1,0:T(8,128)(2,1)} %all-gather.5.cloned.1.call-done, bf16[2048,1024]{1,0:T(8,128)(2,1)} %param.9), kind=kOutput, calls=%fused_computation.20 | convolution fusion | flops 4297064448 | bytes 10485760 | tf_op jit(solution)/shard_map/dot_general | solution.py:22
  115.1 0.0 all-reduce.3.cloned.1.call-update
  115.2 0.0 reduce-scatter.5.cloned.1.call-start
  115.2 103.5 %all-reduce.3.cloned.1.call-done = (bf16[1024,2048]{1,0:T(8,128)(2,1)}, bf16[1024,2048]{1,0:T(8,128)(2,1)}) async-done(((bf16[1024,2048]{1,0:T(8,128)(2,1)}, bf16[1024,2048]{1,0:T(8,128)(2,1)}), (bf16[1024,2048]{1,0:T(8,128)(2,1)}, bf16[1024,2048]{1,0:T(8,128)(2,1)})) %all-reduce.3.cloned.1.call-update) | async-done | bytes 8388624 | tf_op jit(solution)/shard_map/psum | solution.py:17
  218.7 0.0 copy-start.3
  218.7 9.1 %fusion.8 = (bf16[1024,2048]{1,0:T(8,128)(2,1)S(1)}, f32[1024,2048]{1,0:T(8,128)}) fusion(bf16[1024,2048]{1,0:T(8,128)(2,1)} %get-tuple-element.4, bf16[1024,2048]{1,0:T(8,128)(2,1)} %get-tuple-element.5), kind=kLoop, calls=%fused_computation.17 | loop fusion | flops 25165824 | bytes 20971520 | tf_op jit(solution)/shard_map/convert_element_type | solution.py:65
  227.8 0.0 copy-start.2
  227.8 2.0 copy-done.2
  229.8 0.0 copy-done.3
  229.8 5.7 %convolution_convert_fusion.4 = bf16[1024,1024]{1,0:T(8,128)(2,1)} fusion(bf16[1024,2048]{1,0:T(8,128)(2,1)S(1)} %get-tuple-element.6, bf16[1024,2048]{1,0:T(8,128)(2,1)S(1)} %copy-done.3), kind=kOutput, calls=%fused_computation.22 | convolution fusion | flops 4296015872 | bytes 10485760 | tf_op jit(solution)/shard_map/dot_general | solution.py:22
  235.6 0.0 reduce-scatter.5.cloned.1.call-update
  235.6 0.2 reduce-scatter.3.cloned.1.call-start
  235.8 11.7 %convolution_convert_fusion.5 = bf16[1024,1024]{1,0:T(8,128)(2,1)} fusion(bf16[2048,1024]{1,0:T(8,128)(2,1)} %param.9, f32[1024,2048]{1,0:T(8,128)} %get-tuple-element.7, bf16[1024,2048]{1,0:T(8,128)(2,1)} %get-tuple-element.4), kind=kOutput, calls=%fused_computation.23 | convolution fusion | flops 4302307328 | bytes 18874368 | tf_op jit(solution)/shard_map/dot_general | solution.py:22
  247.5 0.0 reduce-scatter.3.cloned.1.call-update
  247.5 0.0 copy-start.1
  247.5 0.0 copy-start.4
  247.5 9.6 %convolution_convert_fusion.1 = bf16[1024,2048]{1,0:T(8,128)(2,1)} fusion(bf16[1024,1024]{1,0:T(8,128)(2,1)} %all-gather.3.cloned.1.call-done, bf16[1024,2048]{1,0:T(8,128)(2,1)} %copy-done.2), kind=kOutput, calls=%fused_computation.19 | convolution fusion | flops 4297064448 | bytes 10485760 | tf_op jit(solution)/shard_map/dot_general | solution.py:71
  257.1 0.0 copy-done.1
  257.1 0.0 copy-done.4
  257.1 10.0 %convolution_convert_fusion = bf16[2048,1024]{1,0:T(8,128)(2,1)} fusion(bf16[1024,1024]{1,0:T(8,128)(2,1)S(1)} %copy-done.4, f32[1024,2048]{1,0:T(8,128)} %get-tuple-element.7, bf16[1024,2048]{1,0:T(8,128)(2,1)S(1)} %copy-done.1), kind=kOutput, calls=%fused_computation.18 | convolution fusion | flops 4303355904 | bytes 18874368 | tf_op jit(solution)/shard_map/dot_general | solution.py:68
  267.2 42.9 %reduce-scatter.5.cloned.1.call-done = bf16[64,1024]{1,0:T(8,128)(2,1)} async-done(((bf16[1024,1024]{1,0:T(8,128)(2,1)}), bf16[64,1024]{1,0:T(8,128)(2,1)}) %reduce-scatter.5.cloned.1.call-update) | async-done | bytes 131088 | tf_op jit(solution)/shard_map/reduce_scatter | solution.py:45
  310.1 1.8 scatter_custom_fusion.1
  311.9 0.9 convert_element_type.61
  312.8 74.6 %reduce-scatter.3.cloned.1.call-done = bf16[64,1024]{1,0:T(8,128)(2,1)} async-done(((bf16[1024,1024]{1,0:T(8,128)(2,1)}), bf16[64,1024]{1,0:T(8,128)(2,1)}) %reduce-scatter.3.cloned.1.call-update) | async-done | bytes 131088 | tf_op jit(solution)/shard_map/reduce_scatter | solution.py:45
  387.3 1.8 scatter_custom_fusion
  389.1 0.9 convert_element_type.53
  (2 shorter events, 0.0 us)
Async XLA Ops:
  7.2 1.4 copy-start
  7.2 51.3 %all-gather.3.cloned.1.call-start = ((), (), s32[]{:S(2)}) async-start(), calls=%async_computation.2 | async-start | bytes 2228224 | tf_op jit(solution)/shard_map/all_gather | solution.py:41
  10.1 95.7 %all-gather.5.cloned.1.call-start = ((), (), s32[]{:S(2)}) async-start(), calls=%async_computation.4 | async-start | bytes 2228224 | tf_op jit(solution)/shard_map/all_gather | solution.py:61
  13.5 205.3 %all-reduce.3.cloned.1.call-start = ((), (), s32[]{:S(2)}) async-start(), calls=%async_computation.6 | async-start | bytes 16777216 | tf_op jit(solution)/shard_map/psum | solution.py:17
  115.2 194.9 %reduce-scatter.5.cloned.1.call-start = ((), (), s32[]{:S(2)}) async-start(), calls=%async_computation.5 | async-start | bytes 2228224 | tf_op jit(solution)/shard_map/reduce_scatter | solution.py:45
  218.7 11.1 %copy-start.3 = (bf16[1024,2048]{1,0:T(8,128)(2,1)S(1)}, bf16[1024,2048]{1,0:T(8,128)(2,1)}, u32[]{:S(2)}) copy-start(bf16[1024,2048]{1,0:T(8,128)(2,1)} %param.8) | copy-start | bytes 12582916
  227.8 2.0 copy-start.2
  235.6 151.7 %reduce-scatter.3.cloned.1.call-start = ((), (), s32[]{:S(2)}) async-start(), calls=%async_computation.3 | async-start | bytes 2228224 | tf_op jit(solution)/shard_map/reduce_scatter | solution.py:45
  247.5 9.6 %copy-start.1 = (bf16[1024,2048]{1,0:T(8,128)(2,1)S(1)}, bf16[1024,2048]{1,0:T(8,128)(2,1)}, u32[]{:S(2)}) copy-start(bf16[1024,2048]{1,0:T(8,128)(2,1)} %get-tuple-element.4) | copy-start | bytes 12582916
  247.5 9.6 %copy-start.4 = (bf16[1024,1024]{1,0:T(8,128)(2,1)S(1)}, bf16[1024,1024]{1,0:T(8,128)(2,1)}, u32[]{:S(2)}) copy-start(bf16[1024,1024]{1,0:T(8,128)(2,1)} %all-gather.5.cloned.1.call-done) | copy-start | bytes 6291460
Sparse Core Ops, SparseCore 0:
  10.7 47.7 all-gather.2
  61.2 44.5 all-gather.4
  115.3 103.4 all-reduce.2
  235.7 74.3 reduce-scatter.4
  313.5 73.7 reduce-scatter.2
where the time goes:
time: 397 us
  waiting for transfers between devices  304 us (77%)
  matrix products  55.7 us (14%)
  other arithmetic  17.3 us (4%)
  between operations  14.5 us (4%)
  local copies, waits for them, and re-layouts  4.65 us (1%)
    reduce_scatter x2, waiting for transfers between devices, send_home(): lax.psum_scatter(contract_rows(left_side, right_side, flip_axis).astype(j...  117 us
    psum x1, waiting for transfers between devices, hidden_rows(): summed = lax.psum(part_rows, 'expert').astype(jnp.float32)  104 us
    all_gather x1, waiting for transfers between devices, local(): piece_rows = lax.all_gather(picked, 'dp', axis=0, tiled=True)  45 us
    all_gather x1, waiting for transfers between devices, local(): back_piece_rows = lax.all_gather(grad_pick, 'dp', axis=0, tiled=True)  37.9 us
    dot_general x3, matrix products, contract_rows(): lax.dot_general(left_side, right_side, (((1,), (flip_axis,)), ((), ())),...  26.8 us
    dot_general x1, matrix products, local(): lax.dot_general(hidden, back_piece_rows, (((0,), (0,)), ((), ())), prefer...  10 us
    dot_general x1, matrix products, local(): lax.dot_general(piece_rows, back_pre, (((0,), (0,)), ((), ())), preferred...  9.57 us
    dot_general x1, matrix products, local(): jnp.dot(piece_rows, w_in, preferred_element_type=jnp.float32)  9.33 us
  transfers between devices with their start and end apart: 5, of which 5 were waited for; matrix products, arithmetic and copies ran while one was open for 12% of the time, Pallas kernels for 0%

commit v1 on v0

v1 whole, which is shorter than its diff:
```python
import jax
import jax.numpy as jnp
from jax import lax
from jax.experimental import pallas as pl
from jax.experimental.pallas import tpu as pltpu
from jax.sharding import PartitionSpec as P

half_root = 0.7071067811865476
inv_root_tau = 0.3989422804014327

MESH = pl.DeviceIdType.MESH
BF = jnp.bfloat16
F32 = jnp.float32

N_COPIES = 240
N_LOCAL = 16

NN = (((1,), (0,)), ((), ()))
NT = (((1,), (1,)), ((), ()))


def dot(a, b, dims=NN):
    return lax.dot_general(a, b, dims, preferred_element_type=F32)


def gelu_pair(pre_act):
    cdf_part = 0.5 * (1.0 + lax.erf(pre_act * half_root))
    slopes = cdf_part + pre_act * jnp.exp(-0.5 * pre_act * pre_act) * inv_root_tau
    return (pre_act * cdf_part, slopes)


def wrap(v):
    return lax.rem(v + 8, 4)


def kernel(
    pick_ref, gate_ref, count_ref, tok_hbm, cot_hbm, wi_hbm, wo_hbm,
    rows_out, hb_out, slots_out,
    tok, cot, wi, wo, ag, cnt, c_mat, ct, rows, xs, xr, ps, opp_rx, nbr_rx, acc, slope, hb,
    part, spread, f_opp, f_nbr, grouped, s_opp, s_nbr,
    send_sem, recv_sem, local_sem,
):
    dp, ex = lax.axis_index("dp"), lax.axis_index("expert")
    x, z = lax.div(dp, 4), lax.rem(dp, 4)
    y, c = lax.div(ex, 2), lax.rem(ex, 2)
    oc = 1 - c
    dev_x = {1: (wrap(x + 1) * 4 + z, ex), -1: (wrap(x - 1) * 4 + z, ex)}
    dev_z = {1: (x * 4 + wrap(z + 1), ex), -1: (x * 4 + wrap(z - 1), ex)}
    dev_y = {1: (dp, wrap(y + 1) * 2 + c), -1: (dp, wrap(y - 1) * 2 + c)}
    dev_c = (dp, y * 2 + oc)

    counter = [0]
    sent = []

    def fresh(n=1):
        first = counter[0]
        counter[0] += n
        assert counter[0] <= N_COPIES
        return first

    def copy(i, src, dst, dev):
        return pltpu.make_async_remote_copy(
            src_ref=src, dst_ref=dst, send_sem=send_sem.at[i], recv_sem=recv_sem.at[i],
            device_id=dev, device_id_type=MESH,
        )

    def send(i, src, dst, dev):
        d = copy(i, src, dst, dev)
        d.start()
        sent.append(d)

    def recv(i, landing, dev):
        copy(i, landing, landing, dev).wait_recv()

    locals_open = []

    def local(src, dst):
        d = pltpu.make_async_copy(src, dst, local_sem.at[len(locals_open)])
        d.start()
        locals_open.append(d)
        return d

    load_tok = local(tok_hbm, tok)
    load_cot = local(cot_hbm, cot)
    load_wi = local(wi_hbm, wi)
    load_wo = local(wo_hbm, wo)

    barrier = pltpu.get_barrier_semaphore()
    for dev in (dev_x[1], dev_x[-1], dev_z[1], dev_z[-1], dev_y[1], dev_y[-1], dev_c):
        pl.semaphore_signal(barrier, inc=1, device_id=dev, device_id_type=MESH)

    def pick(t):
        if t == 0:
            load_tok.wait()
            got = dot(pick_ref[...], tok[...]).astype(BF)
        else:
            load_cot.wait()
            got = (gate_ref[:, 0:1] * dot(pick_ref[...], cot[...])).astype(BF)
        for ph in range(2):
            for h in range(2):
                ag[t, ph, h, x, z] = got[32 * ph:32 * ph + 32, 512 * h:512 * h + 512]

    class Gather:
        def __init__(self, buf, h, lead):
            self.buf, self.h, self.lead = buf, h, lead
            self.f, self.s = (x, z) if h == 0 else (z, x)
            self.fd, self.sd = (dev_x, dev_z) if h == 0 else (dev_z, dev_x)
            self.i = fresh(8)

        def blk(self, fi, si):
            where = (fi, si) if self.h == 0 else (si, fi)
            return self.buf.at[self.lead + where]

        def grp(self, si, first, n):
            where = (pl.ds(first, n), si) if self.h == 0 else (si, pl.ds(first, n))
            return self.buf.at[self.lead + where]

        def s1(self):
            b = self.blk(self.f, self.s)
            send(self.i, b, b, self.fd[1])
            send(self.i + 1, b, b, self.fd[-1])

        def s2(self):
            for n, d in ((0, 1), (1, -1)):
                b = self.blk(wrap(self.f - d), self.s)
                recv(self.i + n, b, self.fd[d])
                b = b.at[pl.ds(16 * n, 16)]
                send(self.i + 2 + n, b, b, self.fd[d])

        def s4(self):
            for n, d in ((0, 1), (1, -1)):
                b = self.blk(wrap(self.f + 2), self.s).at[pl.ds(16 * n, 16)]
                recv(self.i + 2 + n, b, self.fd[d])
            g = self.grp(self.s, 0, 4)
            send(self.i + 4, g, g, self.sd[1])
            send(self.i + 5, g, g, self.sd[-1])

        def s5(self):
            for n, d in ((0, 1), (1, -1)):
                recv(self.i + 4 + n, self.grp(wrap(self.s - d), 0, 4), self.sd[d])
                g = self.grp(wrap(self.s - d), 2 * n, 2)
                send(self.i + 6 + n, g, g, self.sd[d])

        def s6(self):
            for n, d in ((0, 1), (1, -1)):
                recv(self.i + 6 + n, self.grp(wrap(self.s + 2), 2 * n, 2), self.sd[d])

    class Counts:
        def __init__(self):
            self.i = fresh(6)

        def s1(self):
            b = cnt.at[x, z]
            send(self.i, b, b, dev_x[1])
            send(self.i + 1, b, b, dev_x[-1])

        def s2(self):
            recv(self.i, cnt.at[wrap(x - 1), z], dev_x[1])
            recv(self.i + 1, cnt.at[wrap(x + 1), z], dev_x[-1])
            b = cnt.at[wrap(x - 1), z]
            send(self.i + 2, b, b, dev_x[1])

        def s4(self):
            recv(self.i + 2, cnt.at[wrap(x + 2), z], dev_x[1])
            b = cnt.at[:, z]
            send(self.i + 3, b, b, dev_z[1])
            send(self.i + 4, b, b, dev_z[-1])

        def s5(self):
            recv(self.i + 3, cnt.at[:, wrap(z - 1)], dev_z[1])
            recv(self.i + 4, cnt.at[:, wrap(z + 1)], dev_z[-1])
            b = cnt.at[:, wrap(z - 1)]
            send(self.i + 5, b, b, dev_z[1])

        def s6(self):
            recv(self.i + 5, cnt.at[:, wrap(z + 2)], dev_z[1])

    class Both:
        def __init__(self, t, ph):
            self.parts = [Gather(ag, h, (t, ph, h)) for h in range(2)]

        def __getattr__(self, name):
            return lambda: [getattr(p, name)() for p in self.parts]

    def places():
        first, second = [], []
        total = jnp.zeros((8, 128), jnp.int32)
        for i in range(16):
            held = jnp.minimum(cnt[i // 4, i % 4], 32)
            first.append((total, held))
            total = total + held
        for i in range(16):
            held = jnp.maximum(cnt[i // 4, i % 4] - 32, 0)
            second.append((total, held))
            total = total + held
        return first, second

    def lane_places(shards):
        lane = lax.broadcasted_iota(jnp.int32, (8, 128), 1)
        quarter, slot = lane // 32, lane % 32
        tiles = []
        for b in range(4):
            start, held = shards[4 * b + 3]
            for j in (2, 1, 0):
                start = jnp.where(quarter == j, shards[4 * b + j][0], start)
                held = jnp.where(quarter == j, shards[4 * b + j][1], held)
            tiles.append(jnp.where(slot < held, start + slot, -1))
        return tiles

    def build_c():
        first, second = places()
        row = lax.broadcasted_iota(jnp.int32, (256, 128), 0)
        for n, (shards, k) in enumerate(((first, 0), (first, 1), (second, 1))):
            for b, tile in enumerate(lane_places(shards)):
                hit = jnp.broadcast_to(tile[0:1], (256, 128)) == row + 256 * k
                c_mat[n, :, 128 * b:128 * b + 128] = jnp.where(hit, 1.0, 0.0).astype(BF)

    def build_ct():
        first, second = places()
        slot = lax.broadcasted_iota(jnp.int32, (32, 128), 0)
        lane = lax.broadcasted_iota(jnp.int32, (32, 128), 1)
        for i in range(16):
            for ph, shards in ((0, first), (1, second)):
                start = jnp.broadcast_to(shards[i][0][0:1], (32, 128))
                held = jnp.broadcast_to(shards[i][1][0:1], (32, 128))
                place = jnp.where(slot < held, start + slot, -1)
                for b in range(4):
                    hit = place == lane + 128 * b
                    ct[i // 4, i % 4, 32 * ph:32 * ph + 32, 128 * b:128 * b + 128] = jnp.where(
                        hit, 1.0, 0.0
                    ).astype(BF)

    def compact(t, k):
        for h in range(2):
            if k == 0:
                got = dot(c_mat[0], ag[t, 0, h].reshape(512, 512))
            else:
                got = dot(c_mat[1], ag[t, 0, h].reshape(512, 512))
                got += dot(c_mat[2], ag[t, 1, h].reshape(512, 512))
            rows[t, 256 * k:256 * k + 256, 512 * h:512 * h + 512] = got.astype(BF)

    def hidden_cols(core, yy):
        return pl.ds(pl.multiple_of(core * 1024 + yy * 256, 256), 256)

    class Reduce:
        def __init__(self, t, k):
            self.t, self.k = t, k
            self.ic, self.io, self.inb = fresh(4), fresh(2), fresh(2)

        def tile(self, core, yy):
            left = rows[self.t, 256 * self.k:256 * self.k + 256, :]
            if self.t == 0:
                return dot(left, wi[:, hidden_cols(core, yy)])
            return dot(left, wo[hidden_cols(core, yy), :], NT)

        def m1(self):
            t, k = self.t, self.k

            def step(j, carry):
                yy = wrap(y + 2 - j)
                xs[t, k, yy] = self.tile(oc, yy).astype(BF)
                copy(self.ic + yy, xs.at[t, k, yy], xr.at[t, k, yy], dev_c).start()
                return carry

            lax.fori_loop(0, 4, step, 0)

        def own_tile(self, yy):
            t, k = self.t, self.k
            got = self.tile(c, yy)
            copy(self.ic + yy, xs.at[t, k, yy], xr.at[t, k, yy], dev_c).wait_recv()
            return got + xr[t, k, yy].astype(F32)

        def m2(self):
            t, k = self.t, self.k
            ps[t, k, 0] = self.own_tile(wrap(y + 2)).astype(BF)
            for n, d in ((0, 1), (1, -1)):
                send(
                    self.io + n, ps.at[t, k, 0, pl.ds(128 * n, 128)], opp_rx.at[t, k, n], dev_y[d]
                )

            def step(j, carry):
                acc[t, k, j - 1] = self.own_tile(wrap(y + 2 - j))
                return carry

            lax.fori_loop(1, 4, step, 0)

        def nbr(self):
            t, k = self.t, self.k
            for n, d in ((0, 1), (1, -1)):
                recv(self.io + n, opp_rx.at[t, k, n], dev_y[d])
                here = pl.ds(128 * n, 128)
                away = pl.ds(128 * (1 - n), 128)
                j = 0 if d == 1 else 2
                ps[t, k, 1 + n, here] = (
                    acc[t, k, j, here] + opp_rx[t, k, n].astype(F32)
                ).astype(BF)
                ps[t, k, 1 + n, away] = acc[t, k, j, away].astype(BF)
                send(self.inb + n, ps.at[t, k, 1 + n], nbr_rx.at[t, k, n], dev_y[d])

        def total(self):
            t, k = self.t, self.k
            for n, d in ((0, 1), (1, -1)):
                recv(self.inb + n, nbr_rx.at[t, k, n], dev_y[d])
            return acc[t, k, 1] + nbr_rx[t, k, 0].astype(F32) + nbr_rx[t, k, 1].astype(F32)

        def wait_sent(self):
            t, k = self.t, self.k

            def step(yy, carry):
                copy(self.ic + yy, xs.at[t, k, yy], xr.at[t, k, yy], dev_c).wait_send()
                return carry

            lax.fori_loop(0, 4, step, 0)

    class Share:
        def __init__(self, t, k):
            self.t, self.k = t, k
            self.iy, self.io, self.ic = fresh(2), fresh(2), fresh(4)

        def piece(self, core, yy):
            return hb.at[self.t, pl.ds(256 * self.k, 256), hidden_cols(core, yy)]

        def half(self, core, yy, n):
            return hb.at[self.t, pl.ds(256 * self.k + 128 * n, 128), hidden_cols(core, yy)]

        def own(self, value):
            hb[self.t, pl.ds(256 * self.k, 256), hidden_cols(c, y)] = value.astype(BF)
            p = self.piece(c, y)
            send(self.iy, p, p, dev_y[1])
            send(self.iy + 1, p, p, dev_y[-1])
            send(self.ic, p, p, dev_c)

        def fwd(self):
            for n, d in ((0, 1), (1, -1)):
                p = self.piece(c, wrap(y - d))
                recv(self.iy + n, p, dev_y[d])
                q = self.half(c, wrap(y - d), n)
                send(self.io + n, q, q, dev_y[d])
                send(self.ic + 1 + n, p, p, dev_c)

        def opp(self):
            for n, d in ((0, 1), (1, -1)):
                recv(self.io + n, self.half(c, wrap(y + 2), n), dev_y[d])
            p = self.piece(c, wrap(y + 2))
            send(self.ic + 3, p, p, dev_c)

        def done(self):
            for n, yy in enumerate((y, wrap(y - 1), wrap(y + 1), wrap(y + 2))):
                recv(self.ic + n, self.piece(oc, yy), dev_c)

    def contract(t, k):
        def step(n, carry):
            cols = pl.ds(pl.multiple_of(n * 256, 256), 256)
            left = hb[t, 256 * k:256 * k + 256, :]
            got = dot(left, wo[:, cols]) if t == 0 else dot(left, wi[cols, :], NT)
            part[t, 256 * k:256 * k + 256, cols] = got.astype(BF)
            return carry

        lax.fori_loop(0, 4, step, 0)

    class Home:
        def __init__(self, t, h):
            self.t, self.h = t, h
            self.f, self.s = (x, z) if h == 0 else (z, x)
            self.fd, self.sd = (dev_x, dev_z) if h == 0 else (dev_z, dev_x)
            self.i = fresh(8)

        def group(self, fi):
            picks = ct[fi] if self.h == 0 else ct[:, fi]
            got = dot(picks.reshape(256, 512), part[self.t, :, 512 * self.h:512 * self.h + 512])
            return got.reshape(4, 64, 512)

        def f1(self):
            t, h = self.t, self.h
            spread[t, h, 0] = self.group(wrap(self.f + 2)).astype(BF)
            for n, d in ((0, 1), (1, -1)):
                send(
                    self.i + n, spread.at[t, h, 0, pl.ds(2 * n, 2)], f_opp.at[t, h, n], self.fd[d]
                )

        def f2(self):
            t, h = self.t, self.h
            for n, d in ((0, 1), (1, -1)):
                got = self.group(wrap(self.f + d))
                recv(self.i + n, f_opp.at[t, h, n], self.fd[d])
                near = got[2 * n:2 * n + 2] + f_opp[t, h, n].astype(F32)
                spread[t, h, 1 + n, 2 * n:2 * n + 2] = near.astype(BF)
                spread[t, h, 1 + n, 2 - 2 * n:4 - 2 * n] = got[2 - 2 * n:4 - 2 * n].astype(BF)
                send(self.i + 2 + n, spread.at[t, h, 1 + n], f_nbr.at[t, h, n], self.fd[d])

        def f3(self):
            t, h = self.t, self.h
            got = self.group(self.f)
            for n, d in ((0, 1), (1, -1)):
                recv(self.i + 2 + n, f_nbr.at[t, h, n], self.fd[d])
            got = got + f_nbr[t, h, 0].astype(F32) + f_nbr[t, h, 1].astype(F32)
            grouped[t, h] = got.astype(BF)
            far = wrap(self.s + 2)
            for n, d in ((0, 1), (1, -1)):
                send(
                    self.i + 4 + n, grouped.at[t, h, far, pl.ds(32 * n, 32)], s_opp.at[t, h, n],
                    self.sd[d],
                )

        def g2(self):
            t, h = self.t, self.h
            for n, d in ((0, 1), (1, -1)):
                recv(self.i + 4 + n, s_opp.at[t, h, n], self.sd[d])
                to = wrap(self.s + d)
                here = pl.ds(32 * n, 32)
                grouped[t, h, to, here] = (
                    grouped[t, h, to, here].astype(F32) + s_opp[t, h, n].astype(F32)
                ).astype(BF)
                send(self.i + 6 + n, grouped.at[t, h, to], s_nbr.at[t, h, n], self.sd[d])

        def g3(self):
            t, h = self.t, self.h
            for n, d in ((0, 1), (1, -1)):
                recv(self.i + 6 + n, s_nbr.at[t, h, n], self.sd[d])
            got = (
                grouped[t, h, self.s].astype(F32)
                + s_nbr[t, h, 0].astype(F32)
                + s_nbr[t, h, 1].astype(F32)
            )
            if t == 0:
                got = gate_ref[:, 0:1] * got
            slots_out[t, :, 512 * h:512 * h + 512] = got.astype(BF)

    class HomeBoth:
        def __init__(self, t):
            self.parts = [Home(t, h) for h in range(2)]

        def __getattr__(self, name):
            return lambda: [getattr(p, name)() for p in self.parts]

    r_a, r_b, g_a, g_b = Both(0, 0), Both(0, 1), Both(1, 0), Both(1, 1)
    meta = Counts()
    pre = [Reduce(0, 0), Reduce(0, 1)]
    back = [Reduce(1, 0), Reduce(1, 1)]
    hid = [Share(0, 0), Share(0, 1)]
    bpre = [Share(1, 0), Share(1, 1)]
    mixed, d_tok = HomeBoth(0), HomeBoth(1)

    def fin_pre(k):
        activated, slopes = gelu_pair(pre[k].total())
        slope[k] = slopes
        hid[k].own(activated)

    def fin_back(k):
        bpre[k].own(back[k].total() * slope[k])

    cnt[x, z] = count_ref[...]
    pick(0)
    pl.semaphore_wait(barrier, 7)
    r_a.s1()
    meta.s1()
    r_b.s1()
    pick(1)
    r_a.s2()
    meta.s2()
    r_a.s4()
    meta.s4()
    r_b.s2()
    r_a.s5()
    meta.s5()
    r_b.s4()
    meta.s6()
    build_c()
    g_a.s1()
    g_b.s1()
    r_a.s6()
    compact(0, 0)
    load_wi.wait()
    pre[0].m1()
    pre[0].m2()
    r_b.s5()
    g_a.s2()
    g_b.s2()
    g_a.s4()
    pre[0].nbr()
    r_b.s6()
    compact(0, 1)
    pre[1].m1()
    pre[1].m2()
    out_rows = local(rows.at[0], rows_out.at[0])
    g_a.s5()
    g_b.s4()
    fin_pre(0)
    pre[1].nbr()
    g_a.s6()
    compact(1, 0)
    load_wo.wait()
    back[0].m1()
    back[0].m2()
    g_b.s5()
    hid[0].fwd()
    fin_pre(1)
    back[0].nbr()
    g_b.s6()
    compact(1, 1)
    back[1].m1()
    back[1].m2()
    out_grads = local(rows.at[1], rows_out.at[1])
    hid[0].opp()
    hid[1].fwd()
    fin_back(0)
    back[1].nbr()
    build_ct()
    hid[0].done()
    contract(0, 0)
    hid[1].opp()
    bpre[0].fwd()
    hid[1].done()
    out_hid = local(hb.at[0], hb_out.at[0])
    fin_back(1)
    contract(0, 1)
    mixed.f1()
    bpre[0].opp()
    mixed.f2()
    bpre[1].fwd()
    bpre[0].done()
    contract(1, 0)
    mixed.f3()
    bpre[1].opp()
    mixed.g2()
    bpre[1].done()
    out_bp = local(hb.at[1], hb_out.at[1])
    contract(1, 1)
    d_tok.f1()
    mixed.g3()
    d_tok.f2()
    d_tok.f3()
    d_tok.g2()
    d_tok.g3()

    for r in pre + back:
        r.wait_sent()
    for d in sent:
        d.wait_send()
    for d in (out_rows, out_grads, out_hid, out_bp):
        d.wait()


def exchange(pick, gate, count, tokens, cotangent, w_in, w_out):
    vmem = pl.BlockSpec(memory_space=pltpu.VMEM)
    anywhere = pl.BlockSpec(memory_space=pl.ANY)

    def v(*shape, dtype=BF):
        return pltpu.VMEM(shape, dtype)

    return pl.pallas_call(
        kernel,
        out_shape=(
            jax.ShapeDtypeStruct((2, 512, 1024), BF),
            jax.ShapeDtypeStruct((2, 512, 2048), BF),
            jax.ShapeDtypeStruct((2, 64, 1024), BF),
        ),
        in_specs=[vmem] * 3 + [anywhere] * 4,
        out_specs=(anywhere, anywhere, vmem),
        scratch_shapes=[
            v(256, 1024), v(256, 1024), v(1024, 2048), v(2048, 1024),
            v(2, 2, 2, 4, 4, 32, 512),
            v(4, 4, 8, 128, dtype=jnp.int32),
            v(3, 256, 512),
            v(4, 4, 64, 512),
            v(2, 512, 1024),
            v(2, 2, 4, 256, 256), v(2, 2, 4, 256, 256),
            v(2, 2, 3, 256, 256),
            v(2, 2, 2, 128, 256),
            v(2, 2, 2, 256, 256),
            v(2, 2, 3, 256, 256, dtype=F32),
            v(2, 256, 256, dtype=F32),
            v(2, 512, 2048),
            v(2, 512, 1024),
            v(2, 2, 3, 4, 64, 512),
            v(2, 2, 2, 2, 64, 512),
            v(2, 2, 2, 4, 64, 512),
            v(2, 2, 4, 64, 512),
            v(2, 2, 2, 32, 512),
            v(2, 2, 2, 64, 512),
            pltpu.SemaphoreType.DMA((N_COPIES,)),
            pltpu.SemaphoreType.DMA((N_COPIES,)),
            pltpu.SemaphoreType.DMA((N_LOCAL,)),
        ],
        compiler_params=pltpu.CompilerParams(
            collective_id=0, has_side_effects=True, vmem_limit_bytes=60 * 2**20
        ),
        cost_estimate=pl.CostEstimate(
            flops=10 * 10**9, bytes_accessed=20 * 2**20, transcendentals=2**19
        ),
    )(pick, gate, count, tokens, cotangent, w_in, w_out)


def local(tokens, w_in, w_out, chosen, counts, gates, cotangent):
    places = chosen[0]
    live = jnp.arange(64) < counts[0]
    spots = jnp.arange(256)
    pick = ((places[:, None] == spots[None, :]) & live[:, None]).astype(BF)
    gate = jnp.broadcast_to(gates[0][:, None], (64, 128))
    count = jnp.broadcast_to(counts[0], (8, 128))
    rows, hb, slots = exchange(pick, gate, count, tokens, cotangent, w_in, w_out)

    def tall(a, b):
        return lax.dot_general(
            a, b, (((0,), (0,)), ((), ())), preferred_element_type=F32
        ).astype(BF)

    return (
        tall(pick, slots[0]),
        tall(pick, slots[1]),
        tall(rows[0], hb[1]),
        tall(hb[0], rows[1]),
    )


def solution(mesh):
    in_specs = (
        P("dp", "expert"),
        P("expert", "dp"),
        P("dp", "expert"),
        P("dp", None),
        P("dp"),
        P("dp", None),
        P("dp", "expert"),
    )
    out_specs = (P("dp", "expert"), P("dp", "expert"), P("expert", "dp"), P("dp", "expert"))
    return jax.shard_map(local, mesh=mesh, in_specs=in_specs, out_specs=out_specs, check_vma=False)
```

time: 397 us -> 128 us (0.32)
  waiting for transfers between devices: 304 us -> 0 us
  Pallas kernels: 0 us -> 110 us
  matrix products: 55.7 us -> 13.2 us
  other arithmetic: 17.3 us -> 1.36 us
  between operations: 14.5 us -> 1.32 us
    reduce_scatter x2 -> x0, waiting for transfers between devices: 117 us -> none  [send_home(): lax.psum_scatter(contract_rows(left_side, right_side, flip_axis).astype(j...]
    pallas_call x0 -> x1, Pallas kernels: none -> 110 us  [exchange(): pl.pallas_call(kernel, out_shape=(jax.ShapeDtypeStruct((2, 512, 1024), BF...]
    psum x1 -> x0, waiting for transfers between devices: 104 us -> none  [hidden_rows(): summed = lax.psum(part_rows, 'expert').astype(jnp.float32)]
    all_gather x2 -> x0, waiting for transfers between devices: 82.9 us -> none  [the longest x1 45 us: local(): piece_rows = lax.all_gather(picked, 'dp', axis=0, tiled=True)]
    dot_general x6 -> x4, matrix products: 55.7 us -> 13.2 us  [tall(): lax.dot_general(a, b, (((0,), (0,)), ((), ())), preferred_element_type=F32)]
    convert_element_type x4 -> x1, other arithmetic: 11.6 us -> 1.36 us  [local(): pick = ((places[:, None] == spots[None, :]) & live[:, None]).astype(BF)]
  transfers between devices with their start and end apart: 5 -> 0, of which waited for: 5 -> 0; matrix products, arithmetic and copies ran while one was open for 12% -> 0% of each run, Pallas kernels for 0% -> 0%
where the time goes in v1:
time: 128 us
  Pallas kernels  110 us (86%)
  matrix products  13.2 us (10%)
  local copies, waits for them, and re-layouts  1.95 us (2%)
  other arithmetic  1.36 us (1%)
  between operations  1.32 us (1%)
    pallas_call x1, Pallas kernels, exchange(): pl.pallas_call(kernel, out_shape=(jax.ShapeDtypeStruct((2, 512, 1024), BF...  110 us
    dot_general x4, matrix products, tall(): lax.dot_general(a, b, (((0,), (0,)), ((), ())), preferred_element_type=F32)  13.2 us

profile of v1, /device:TPU:0, one launch (start us, length us, event | category | flops | bytes accessed | tf_op | source)
XLA Modules:
  0.0 128.2 jit_solution(7519821923046014746)
XLA Ops:
  1.3 1.4 %fusion.15.pick_ref = bf16[64,256]{1,0:T(8,128)(2,1)} fusion(s32[64]{0:T(128)} %bitcast.23, pred[64]{0:T(512)(128)(4,1)S(1)} %iota_compare_fusion.1), kind=kLoop, calls=%fused_computation.18 | loop fusion | flops 49152 | bytes 33088 | tf_op jit(solution)/shard_map/convert_element_type | solution.py:598
  2.6 0.6 broadcast_in_dim.14.count_ref
  3.2 1.3 %broadcast_in_dim.13.gate_ref = f32[64,128]{1,0:T(8,128)} broadcast(f32[64]{0:T(128)} %bitcast.26), dimensions={0} | broadcast | bytes 33024 | tf_op jit(solution)/shard_map/broadcast_in_dim | solution.py:599
  4.6 110.4 %shard_map.102 = (bf16[2,512,1024]{2,1,0:T(8,128)(2,1)}, bf16[2,512,2048]{2,1,0:T(8,128)(2,1)}, bf16[2,64,1024]{2,1,0:T(8,128)(2,1)}) custom-call(bf16[64,256]{1,0:T(8,128)(2,1)} %fusion.15.pick_ref, f32[64,128]{1,0:T(8,128)} %broadcast_in_dim.13.gate_ref, s32[8,128]{1,0:T(8,128)} %broadcast_in_dim.14.count_ref, bf16[256,1024]{1,0:T(8,128)(2,1)} %tok_hbm.1, ...), custom_call_target="tpu_custom_call" | custom-call | flops 10000000000 | bytes 20971520 | tf_op jit(solution)/shard_map/pallas_call | solution.py:551
  115.0 0.0 copy-start.2
  115.0 0.0 copy-start.3
  115.0 6.4 %convolution_convert_fusion = bf16[2048,1024]{1,0:T(8,128)(2,1)} fusion(bf16[2,512,2048]{2,1,0:T(8,128)(2,1)} %get-tuple-element.9, bf16[2,512,1024]{2,1,0:T(8,128)(2,1)} %get-tuple-element.8), kind=kOutput, calls=%fused_computation | convolution fusion | flops 2149580800 | bytes 7340032 | tf_op jit(solution)/shard_map/dot_general | solution.py:604
  121.4 0.0 copy-done.2
  121.4 0.0 copy-done.3
  121.4 0.0 copy-start
  121.4 0.0 copy-start.1
  121.4 4.4 %convolution_convert_fusion.1 = bf16[1024,2048]{1,0:T(8,128)(2,1)} fusion(bf16[2,512,2048]{2,1,0:T(8,128)(2,1)S(1)} %copy-done.2, bf16[2,512,1024]{2,1,0:T(8,128)(2,1)S(1)} %copy-done.3), kind=kOutput, calls=%fused_computation.1 | convolution fusion | flops 2149580800 | bytes 7340032 | tf_op jit(solution)/shard_map/dot_general | solution.py:604
  125.8 0.0 copy-done
  125.8 0.0 copy-done.1
  125.8 1.2 convolution_convert_fusion.2
  127.0 1.2 convolution_convert_fusion.3
  (1 shorter events, 0.0 us)
Async XLA Ops:
  115.0 6.4 %copy-start.2 = (bf16[2,512,2048]{2,1,0:T(8,128)(2,1)S(1)}, bf16[2,512,2048]{2,1,0:T(8,128)(2,1)}, u32[]{:S(2)}) copy-start(bf16[2,512,2048]{2,1,0:T(8,128)(2,1)} %get-tuple-element.9) | copy-start | bytes 12582916
  115.0 6.4 %copy-start.3 = (bf16[2,512,1024]{2,1,0:T(8,128)(2,1)S(1)}, bf16[2,512,1024]{2,1,0:T(8,128)(2,1)}, u32[]{:S(2)}) copy-start(bf16[2,512,1024]{2,1,0:T(8,128)(2,1)} %get-tuple-element.8) | copy-start | bytes 6291460
  121.4 4.4 %copy-start = (bf16[2,64,1024]{2,1,0:T(8,128)(2,1)S(1)}, bf16[2,64,1024]{2,1,0:T(8,128)(2,1)}, u32[]{:S(2)}) copy-start(bf16[2,64,1024]{2,1,0:T(8,128)(2,1)} %get-tuple-element.7) | copy-start | bytes 786436
  121.4 4.4 %copy-start.1 = (s32[1,64]{1,0:T(1,128)S(1)}, s32[1,64]{1,0:T(1,128)}, u32[]{:S(2)}) copy-start(s32[1,64]{1,0:T(1,128)} %param.10) | copy-start | bytes 772

commit v2 on v0

v2 whole, which is shorter than its diff:
```python
import jax
import jax.numpy as jnp
from jax import lax
from jax.experimental import pallas as pl
from jax.experimental.pallas import tpu as pltpu
from jax.sharding import PartitionSpec as P

half_root = 0.7071067811865476
inv_root_tau = 0.3989422804014327

MESH = pl.DeviceIdType.MESH
BF = jnp.bfloat16
F32 = jnp.float32

N_COPIES = 200
N_LOCAL = 24

ORDER = (
    "pick0", "ag1_00", "ag1_01", "pick1", "ag1_10", "meta1", "ag2_00", "ag2_01", "meta2",
    "ag3_00", "ag3_01", "ag1_11", "ag2_10", "meta", "buildc", "ag4_00", "cmp_00", "ma_00",
    "ag4_01", "mb_00", "cmp_01", "ma_01", "mc_00", "mb_01", "md_00", "nb_00", "ag3_10", "mc_01",
    "buildct", "ag2_11", "md_01", "nb_01", "fin_00", "ag3_11", "fin_01", "ag4_10", "cmp_10",
    "ma_10", "ag4_11", "cmp_11", "fwd_00", "ma_11", "mb_10", "mc_10", "mb_11", "mc_11", "fwd_01",
    "opp_00", "md_11", "md_10", "nb_10", "ct_00", "opp_01", "nb_11", "ct_01", "fin_10", "e0_0",
    "e1_0", "fin_11", "dwo0", "fn0_0", "fn1_0", "fwd_10", "e2_0", "dwo1", "fn2_0", "dwo2",
    "fn3_0", "fs0_0", "fwd_11", "fs1_0", "opp_10", "ct1_11", "fs2_0", "opp_11", "ct_10", "ct2_11",
    "e0_1", "e1_1", "fs3_0", "dwi0", "dwo3", "fn0_1", "dwo4", "fn1_1", "g3_0", "fn2_1", "dwo5",
    "dwo6", "fn3_1", "dwi1", "dwi2", "e2_1", "fs0_1", "fs1_1", "fs2_1", "fs3_1", "dwo7", "dwi3",
    "g3_1",
)

NN = (((1,), (0,)), ((), ()))
NT = (((1,), (1,)), ((), ()))
TN = (((0,), (0,)), ((), ()))


def dot(a, b, dims=NN):
    return lax.dot_general(a, b, dims, preferred_element_type=F32)


def gelu_pair(pre_act):
    cdf_part = 0.5 * (1.0 + lax.erf(pre_act * half_root))
    slopes = cdf_part + pre_act * jnp.exp(-0.5 * pre_act * pre_act) * inv_root_tau
    return (pre_act * cdf_part, slopes)


def wrap(v):
    return lax.rem(v + 8, 4)


def kernel(
    chosen_ref, gates_ref, count_ref, tok_hbm, cot_hbm, wi_hbm, wo_hbm,
    pick_out, slots_out, dwi_out, dwo_out,
    tok, cot, wi, wo, gate, ag, cnt, c_mat, ct, rows, xs, xr, ps, opp_rx, nbr_rx, acc, slope, hb,
    sub, part, spread, home, f_opp, f_nbr, grouped, s_rx, dwi, dwo,
    send_sem, recv_sem, local_sem,
):
    dp, ex = lax.axis_index("dp"), lax.axis_index("expert")
    x, z = lax.div(dp, 4), lax.rem(dp, 4)
    y, c = lax.div(ex, 2), lax.rem(ex, 2)
    oc = 1 - c
    dev_x = {d: (wrap(x + d) * 4 + z, ex) for d in (1, -1, 2)}
    dev_z = {d: (x * 4 + wrap(z + d), ex) for d in (1, -1, 2)}
    dev_y = {d: (dp, wrap(y + d) * 2 + c) for d in (1, -1)}
    dev_c = (dp, y * 2 + oc)
    both = ((0, 1), (1, -1))
    three = ((0, 1), (1, -1), (2, 2))

    counter = [0]
    sent = []

    def fresh(n):
        first = counter[0]
        counter[0] += n
        assert counter[0] <= N_COPIES
        return first

    def copy(i, src, dst, dev):
        return pltpu.make_async_remote_copy(
            src_ref=src, dst_ref=dst, send_sem=send_sem.at[i], recv_sem=recv_sem.at[i],
            device_id=dev, device_id_type=MESH,
        )

    def send(i, src, dst, dev):
        d = copy(i, src, dst, dev)
        d.start()
        sent.append(d)

    def recv(i, landing, dev):
        copy(i, landing, landing, dev).wait_recv()

    opened = []

    def local_copy(src, dst):
        d = pltpu.make_async_copy(src, dst, local_sem.at[len(opened)])
        d.start()
        opened.append(d)
        return d

    load = {
        "tok": local_copy(tok_hbm, tok),
        "cot": local_copy(cot_hbm, cot),
        0: local_copy(wi_hbm, wi),
        1: local_copy(wo_hbm, wo),
    }

    barrier = pltpu.get_barrier_semaphore()
    partners = [dev_x[d] for d in dev_x] + [dev_z[d] for d in dev_z] + [dev_y[1], dev_y[-1], dev_c]
    for dev in partners:
        pl.semaphore_signal(barrier, inc=1, device_id=dev, device_id_type=MESH)

    tasks = {}

    def column(row):
        here = lax.broadcasted_iota(jnp.int32, (64, 64), 0)
        there = lax.broadcasted_iota(jnp.int32, (64, 64), 1)
        wide = jnp.broadcast_to(row.astype(F32), (64, 64))
        return jnp.sum(jnp.where(here == there, wide, 0.0), axis=1, keepdims=True)

    def pick0():
        place = jnp.broadcast_to(column(chosen_ref[...]), (64, 256)).astype(jnp.int32)
        spot = lax.broadcasted_iota(jnp.int32, (64, 256), 1)
        slot = lax.broadcasted_iota(jnp.int32, (64, 256), 0)
        held = jnp.broadcast_to(count_ref[0], (64, 256))
        hit = jnp.where(place == spot, 1.0, 0.0) * jnp.where(slot < held, 1.0, 0.0)
        pick_out[...] = hit.astype(BF)
        gate[...] = jnp.broadcast_to(column(gates_ref[...]), (64, 128))
        cnt[x, z] = jnp.broadcast_to(count_ref[0], (8, 128))
        load["tok"].wait()
        keep(0, dot(pick_out[...], tok[...]).astype(BF))

    def pick1():
        load["cot"].wait()
        keep(1, (gate[:, 0:1] * dot(pick_out[...], cot[...])).astype(BF))

    def keep(t, got):
        for ph in range(2):
            for h in range(2):
                ag[t, ph, h, x, z] = got[32 * ph:32 * ph + 32, 512 * h:512 * h + 512]

    tasks["pick0"], tasks["pick1"] = pick0, pick1

    def axes(h):
        return (x, z, dev_x, dev_z) if h == 0 else (z, x, dev_z, dev_x)

    def add_gather(t, ph):
        base = [fresh(7), fresh(7)]

        def blk(h, fi, si):
            return ag.at[(t, ph, h) + ((fi, si) if h == 0 else (si, fi))]

        def grp(h, si, first, n):
            many = pl.ds(first, n)
            return ag.at[(t, ph, h) + ((many, si) if h == 0 else (si, many))]

        def ag1():
            for h in range(2):
                f, s, fd, sd = axes(h)
                for n, d in three:
                    send(base[h] + n, blk(h, f, s), blk(h, f, s), fd[d])

        def ag2():
            for h in range(2):
                f, s, fd, sd = axes(h)
                for n, d in three:
                    recv(base[h] + n, blk(h, wrap(f - d), s), fd[d])
                for n, d in both:
                    send(base[h] + 3 + n, grp(h, s, 0, 4), grp(h, s, 0, 4), sd[d])

        def ag3():
            for h in range(2):
                f, s, fd, sd = axes(h)
                for n, d in both:
                    recv(base[h] + 3 + n, grp(h, wrap(s - d), 0, 4), sd[d])
                    g = grp(h, wrap(s - d), 2 * n, 2)
                    send(base[h] + 5 + n, g, g, sd[d])

        def ag4():
            for h in range(2):
                f, s, fd, sd = axes(h)
                for n, d in both:
                    recv(base[h] + 5 + n, grp(h, wrap(s + 2), 2 * n, 2), sd[d])

        for name, f in (("ag1", ag1), ("ag2", ag2), ("ag3", ag3), ("ag4", ag4)):
            tasks[f"{name}_{t}{ph}"] = f

    meta_base = fresh(6)

    def meta1():
        for n, d in three:
            send(meta_base + n, cnt.at[x, z], cnt.at[x, z], dev_x[d])

    def meta2():
        for n, d in three:
            recv(meta_base + n, cnt.at[wrap(x - d), z], dev_x[d])
        for n, d in three:
            send(meta_base + 3 + n, cnt.at[:, z], cnt.at[:, z], dev_z[d])

    def meta():
        for n, d in three:
            recv(meta_base + 3 + n, cnt.at[:, wrap(z - d)], dev_z[d])

    tasks.update(meta1=meta1, meta2=meta2, meta=meta)

    def places():
        first, second = [], []
        total = jnp.zeros((8, 128), jnp.int32)
        for i in range(16):
            held = jnp.minimum(cnt[i // 4, i % 4], 32)
            first.append((total, held))
            total = total + held
        for i in range(16):
            held = jnp.maximum(cnt[i // 4, i % 4] - 32, 0)
            second.append((total, held))
            total = total + held
        return first, second

    def lane_places(shards):
        lane = lax.broadcasted_iota(jnp.int32, (8, 128), 1)
        quarter, slot = lane // 32, lane % 32
        tiles = []
        for b in range(4):
            start, held = shards[4 * b + 3]
            for j in (2, 1, 0):
                start = jnp.where(quarter == j, shards[4 * b + j][0], start)
                held = jnp.where(quarter == j, shards[4 * b + j][1], held)
            tiles.append(jnp.where(slot < held, start + slot, -1))
        return tiles

    def buildc():
        first, second = places()
        row = lax.broadcasted_iota(jnp.int32, (256, 128), 0)
        for n, (shards, k) in enumerate(((first, 0), (first, 1), (second, 1))):
            for b, tile in enumerate(lane_places(shards)):
                hit = jnp.broadcast_to(tile[0:1], (256, 128)) == row + 256 * k
                c_mat[n, :, 128 * b:128 * b + 128] = jnp.where(hit, 1.0, 0.0).astype(BF)

    def buildct():
        first, second = places()
        slot = lax.broadcasted_iota(jnp.int32, (32, 128), 0)
        lane = lax.broadcasted_iota(jnp.int32, (32, 128), 1)
        for i in range(16):
            for ph, shards in ((0, first), (1, second)):
                start = jnp.broadcast_to(shards[i][0][0:1], (32, 128))
                held = jnp.broadcast_to(shards[i][1][0:1], (32, 128))
                place = jnp.where(slot < held, start + slot, -1)
                for b in range(4):
                    hit = place == lane + 128 * b
                    ct[i // 4, i % 4, 32 * ph:32 * ph + 32, 128 * b:128 * b + 128] = jnp.where(
                        hit, 1.0, 0.0
                    ).astype(BF)

    tasks["buildc"], tasks["buildct"] = buildc, buildct

    def hidden_cols(core, yy, width=256):
        return pl.ds(pl.multiple_of(core * 1024 + yy * width, width), width)

    def add_chunk(t, k):
        mine = pl.ds(256 * k, 256)
        ic, io, inb = fresh(2), fresh(2), fresh(2)
        iy, iw, ih = fresh(2), fresh(2), fresh(4)
        far = lax.div(wrap(y + 2), 2)
        near = 1 - far

        def cmp():
            for h in range(2):
                cols = slice(512 * h, 512 * h + 512)
                got = dot(c_mat[k], ag[t, 0, h].reshape(512, 512))
                if k == 1:
                    got += dot(c_mat[2], ag[t, 1, h].reshape(512, 512))
                rows[t, mine, cols] = got.astype(BF)

        def pair(core, p):
            left = rows[t, mine, :]
            if t == 0:
                return dot(left, wi[:, hidden_cols(core, p, 512)])
            return dot(left, wo[hidden_cols(core, p, 512), :], NT)

        def for_other(p, n):
            got = pair(oc, p).astype(BF)
            xs[t, k, p, 0] = got[:, :256]
            xs[t, k, p, 1] = got[:, 256:]
            send(ic + n, xs.at[t, k, p], xr.at[t, k, p], dev_c)

        def for_self(p, n):
            got = pair(c, p)
            recv(ic + n, xr.at[t, k, p], dev_c)
            acc[t, k, p, 0] = got[:, :256] + xr[t, k, p, 0].astype(F32)
            acc[t, k, p, 1] = got[:, 256:] + xr[t, k, p, 1].astype(F32)

        def tile(yy):
            return (t, k, lax.div(yy, 2), lax.rem(yy, 2))

        def ma():
            if k == 0:
                load[t].wait()
            for_other(far, 0)

        def mb():
            for_self(far, 0)
            ps[t, k, 0] = acc[tile(wrap(y + 2))].astype(BF)
            for n, d in both:
                send(io + n, ps.at[t, k, 0, pl.ds(128 * n, 128)], opp_rx.at[t, k, n], dev_y[d])

        def mc():
            for_other(near, 1)

        def md():
            for_self(near, 1)

        def nb():
            for n, d in both:
                recv(io + n, opp_rx.at[t, k, n], dev_y[d])
                got = acc[tile(wrap(y + d))]
                here = slice(128 * n, 128 * n + 128)
                away = slice(128 - 128 * n, 256 - 128 * n)
                ps[t, k, 1 + n, here] = (got[here] + opp_rx[t, k, n].astype(F32)).astype(BF)
                ps[t, k, 1 + n, away] = got[away].astype(BF)
                send(inb + n, ps.at[t, k, 1 + n], nbr_rx.at[t, k, n], dev_y[d])

        def piece(core, yy):
            return hb.at[t, mine, hidden_cols(core, yy)]

        def half(yy, n):
            return hb.at[t, pl.ds(256 * k + 128 * n, 128), hidden_cols(c, yy)]

        def fin():
            for n, d in both:
                recv(inb + n, nbr_rx.at[t, k, n], dev_y[d])
            total = acc[tile(y)] + nbr_rx[t, k, 0].astype(F32) + nbr_rx[t, k, 1].astype(F32)
            if t == 0:
                total, slopes = gelu_pair(total)
                slope[k] = slopes
            else:
                total = total * slope[k]
            hb[t, mine, hidden_cols(c, y)] = total.astype(BF)
            p = piece(c, y)
            send(iy, p, p, dev_y[1])
            send(iy + 1, p, p, dev_y[-1])
            send(ih, p, p, dev_c)

        def fwd():
            for n, d in both:
                p, q = piece(c, wrap(y - d)), half(wrap(y - d), n)
                recv(iy + n, p, dev_y[d])
                send(iw + n, q, q, dev_y[d])
                send(ih + 1 + n, p, p, dev_c)

        def opp():
            for n, d in both:
                recv(iw + n, half(wrap(y + 2), n), dev_y[d])
            p = piece(c, wrap(y + 2))
            send(ih + 3, p, p, dev_c)

        def near_in():
            for n, yy in enumerate((y, wrap(y - 1), wrap(y + 1))):
                recv(ih + n, piece(oc, yy), dev_c)

        def far_in():
            recv(ih + 3, piece(oc, wrap(y + 2)), dev_c)

        def whole():
            near_in()
            far_in()

            def step(n, carry):
                cols = pl.ds(pl.multiple_of(n * 256, 256), 256)
                left = hb[t, mine, :]
                got = dot(left, wo[:, cols]) if t == 0 else dot(left, wi[cols, :], NT)
                part[t, mine, cols] = got.astype(BF)
                return carry

            lax.fori_loop(0, 4, step, 0)

        def product(core, yy):
            units = hidden_cols(core, yy)
            left = hb[t, mine, units]
            return dot(left, wo[units, :]) if t == 0 else dot(left, wi[:, units], NT)

        def ct1():
            near_in()
            sub[...] = product(c, y)

            def step(n, carry):
                sub[...] += product(lax.rem(c + lax.div(n, 3), 2), wrap(y + 3 + lax.rem(n, 3)))
                return carry

            lax.fori_loop(0, 1, lambda n, carry: step(2, carry), 0)
            lax.fori_loop(3, 6, step, 0)
            lax.fori_loop(0, 1, step, 0)

        def ct2():
            far_in()
            got = sub[...] + product(c, wrap(y + 2)) + product(oc, wrap(y + 2))
            part[t, mine, :] = got.astype(BF)

        for f in (cmp, ma, mb, mc, md, nb, fin, fwd, opp):
            tasks[f"{f.__name__}_{t}{k}"] = f
        if (t, k) == (1, 1):
            tasks["ct1_11"], tasks["ct2_11"] = ct1, ct2
        else:
            tasks[f"ct_{t}{k}"] = whole

    def add_home(t):
        base = [fresh(19), fresh(19)]

        def group(h, fi):
            picks = ct[fi] if h == 0 else ct[:, fi]
            got = dot(picks.reshape(256, 512), part[t, :, 512 * h:512 * h + 512])
            return got.reshape(4, 64, 512)

        def e0():
            for h in range(2):
                f, s, fd, sd = axes(h)
                spread[t, h, 0] = group(h, wrap(f + 2)).astype(BF)
                for q, far in enumerate((2, 1, -1, 0)):
                    to = wrap(s + far)
                    for n, d in both:
                        send(
                            base[h] + 2 * q + n, spread.at[t, h, 0, to, pl.ds(32 * n, 32)],
                            f_opp.at[t, h, q, n], fd[d],
                        )

        def e1():
            for h in range(2):
                f, s, fd, sd = axes(h)
                for n, d in both:
                    spread[t, h, 1 + n] = group(h, wrap(f + d)).astype(BF)

        def e2():
            for h in range(2):
                home[t, h] = group(h, axes(h)[0])

        def fn(q, far):
            def run():
                for h in range(2):
                    f, s, fd, sd = axes(h)
                    to = wrap(s + far)
                    for n, d in both:
                        recv(base[h] + 2 * q + n, f_opp.at[t, h, q, n], fd[d])
                        here = slice(32 * n, 32 * n + 32)
                        spread[t, h, 1 + n, to, here] = (
                            spread[t, h, 1 + n, to, here].astype(F32)
                            + f_opp[t, h, q, n].astype(F32)
                        ).astype(BF)
                        send(
                            base[h] + 8 + 2 * q + n, spread.at[t, h, 1 + n, to],
                            f_nbr.at[t, h, q, n], fd[d],
                        )
            return run

        def fs(q, far):
            def run():
                for h in range(2):
                    f, s, fd, sd = axes(h)
                    to = wrap(s + far)
                    for n, d in both:
                        recv(base[h] + 8 + 2 * q + n, f_nbr.at[t, h, q, n], fd[d])
                    got = (
                        home[t, h, to]
                        + f_nbr[t, h, q, 0].astype(F32)
                        + f_nbr[t, h, q, 1].astype(F32)
                    )
                    if q == 3:
                        home[t, h, to] = got
                    else:
                        grouped[t, h, q] = got.astype(BF)
                        send(
                            base[h] + 16 + q, grouped.at[t, h, q], s_rx.at[t, h, q], sd[far]
                        )
            return run

        def g3():
            for h in range(2):
                f, s, fd, sd = axes(h)
                got = home[t, h, s]
                for q, far in enumerate((2, 1, -1)):
                    recv(base[h] + 16 + q, s_rx.at[t, h, q], sd[far])
                    got = got + s_rx[t, h, q].astype(F32)
                if t == 0:
                    got = gate[:, 0:1] * got
                slots_out[t, :, 512 * h:512 * h + 512] = got.astype(BF)

        for f in (e0, e1, e2, g3):
            tasks[f"{f.__name__}_{t}"] = f
        for q, far in enumerate((2, 1, -1, 0)):
            tasks[f"fn{q}_{t}"] = fn(q, far)
            tasks[f"fs{q}_{t}"] = fs(q, far)

    def dwo_tile(j):
        def run():
            here = pl.ds(256 * j, 256)
            dwo[here, :] = dot(hb[0, :, here], rows[1], TN).astype(BF)
            local_copy(dwo.at[here], dwo_out.at[here])
        return run

    def dwi_tile(j):
        def run():
            here = pl.ds(256 * j, 256)
            dwi[here, :] = dot(rows[0, :, here], hb[1], TN).astype(BF)
            local_copy(dwi.at[here], dwi_out.at[here])
        return run

    for j in range(8):
        tasks[f"dwo{j}"] = dwo_tile(j)
    for j in range(4):
        tasks[f"dwi{j}"] = dwi_tile(j)
    for t in range(2):
        for i in range(2):
            add_gather(t, i)
            add_chunk(t, i)
        add_home(t)

    entered = False
    for name in ORDER:
        if name == "ag1_00":
            pl.semaphore_wait(barrier, len(partners))
            entered = True
        assert entered or name.startswith("pick")
        tasks.pop(name)()
    assert not tasks

    for d in sent:
        d.wait_send()
    for d in opened[4:]:
        d.wait()


def exchange(chosen, gates, counts, tokens, cotangent, w_in, w_out):
    vmem = pl.BlockSpec(memory_space=pltpu.VMEM)
    smem = pl.BlockSpec(memory_space=pltpu.SMEM)
    anywhere = pl.BlockSpec(memory_space=pl.ANY)

    def v(*shape, dtype=BF):
        return pltpu.VMEM(shape, dtype)

    return pl.pallas_call(
        kernel,
        out_shape=(
            jax.ShapeDtypeStruct((64, 256), BF),
            jax.ShapeDtypeStruct((2, 64, 1024), BF),
            jax.ShapeDtypeStruct((1024, 2048), BF),
            jax.ShapeDtypeStruct((2048, 1024), BF),
        ),
        in_specs=[vmem, vmem, smem] + [anywhere] * 4,
        out_specs=(vmem, vmem, anywhere, anywhere),
        scratch_shapes=[
            v(256, 1024), v(256, 1024), v(1024, 2048), v(2048, 1024),
            v(64, 128, dtype=F32),
            v(2, 2, 2, 4, 4, 32, 512),
            v(4, 4, 8, 128, dtype=jnp.int32),
            v(3, 256, 512),
            v(4, 4, 64, 512),
            v(2, 512, 1024),
            v(2, 2, 2, 2, 256, 256), v(2, 2, 2, 2, 256, 256),
            v(2, 2, 3, 256, 256),
            v(2, 2, 2, 128, 256),
            v(2, 2, 2, 256, 256),
            v(2, 2, 2, 2, 256, 256, dtype=F32),
            v(2, 256, 256, dtype=F32),
            v(2, 512, 2048),
            v(256, 1024, dtype=F32),
            v(2, 512, 1024),
            v(2, 2, 3, 4, 64, 512),
            v(2, 2, 4, 64, 512, dtype=F32),
            v(2, 2, 4, 2, 32, 512),
            v(2, 2, 4, 2, 64, 512),
            v(2, 2, 3, 64, 512),
            v(2, 2, 3, 64, 512),
            v(1024, 2048), v(2048, 1024),
            pltpu.SemaphoreType.DMA((N_COPIES,)),
            pltpu.SemaphoreType.DMA((N_COPIES,)),
            pltpu.SemaphoreType.DMA((N_LOCAL,)),
        ],
        compiler_params=pltpu.CompilerParams(
            collective_id=0, has_side_effects=True, vmem_limit_bytes=62 * 2**20
        ),
        cost_estimate=pl.CostEstimate(
            flops=14 * 10**9, bytes_accessed=20 * 2**20, transcendentals=2**19
        ),
    )(chosen, gates, counts, tokens, cotangent, w_in, w_out)


def local(tokens, w_in, w_out, chosen, counts, gates, cotangent):
    pick, slots, d_w_in, d_w_out = exchange(
        chosen, gates, counts, tokens, cotangent, w_in, w_out
    )

    def scatter(rows):
        return dot(pick, rows, TN).astype(BF)

    return scatter(slots[0]), scatter(slots[1]), d_w_in, d_w_out


def solution(mesh):
    in_specs = (
        P("dp", "expert"),
        P("expert", "dp"),
        P("dp", "expert"),
        P("dp", None),
        P("dp"),
        P("dp", None),
        P("dp", "expert"),
    )
    out_specs = (P("dp", "expert"), P("dp", "expert"), P("expert", "dp"), P("dp", "expert"))
    return jax.shard_map(local, mesh=mesh, in_specs=in_specs, out_specs=out_specs, check_vma=False)
```

time: 397 us -> 100 us (0.25)
  waiting for transfers between devices: 304 us -> 0 us
  Pallas kernels: 0 us -> 87.5 us
  matrix products: 55.7 us -> 4.07 us
  other arithmetic: 17.3 us -> 0 us
  between operations: 14.5 us -> 1.29 us
    reduce_scatter x2 -> x0, waiting for transfers between devices: 117 us -> none  [send_home(): lax.psum_scatter(contract_rows(left_side, right_side, flip_axis).astype(j...]
    psum x1 -> x0, waiting for transfers between devices: 104 us -> none  [hidden_rows(): summed = lax.psum(part_rows, 'expert').astype(jnp.float32)]
    pallas_call x0 -> x1, Pallas kernels: none -> 87.5 us  [exchange(): pl.pallas_call(kernel, out_shape=(jax.ShapeDtypeStruct((64, 256), BF), ja...]
    all_gather x2 -> x0, waiting for transfers between devices: 82.9 us -> none  [the longest x1 45 us: local(): piece_rows = lax.all_gather(picked, 'dp', axis=0, tiled=True)]
    dot_general x6 -> x2, matrix products: 55.7 us -> 4.07 us  [dot(): return lax.dot_general(a, b, dims, preferred_element_type=F32)]
    convert_element_type x4 -> x0, other arithmetic: 11.6 us -> none  [the longest x1 9.07 us: backward_finish(): return ((back_hidden * slopes).astype(jnp.bfloat16), slopes)]
    unnamed x10 -> x4, local copies, waits for them, and re-layouts: 2.03 us -> 6.95 us
  transfers between devices with their start and end apart: 5 -> 0, of which waited for: 5 -> 0; matrix products, arithmetic and copies ran while one was open for 12% -> 0% of each run, Pallas kernels for 0% -> 0%
where the time goes in v2:
time: 100 us; the launch traced here: 99.8 us
  Pallas kernels  87.5 us (88%)
  local copies, waits for them, and re-layouts  6.95 us (7%)
  matrix products  4.07 us (4%)
  between operations  1.29 us (1%)
    pallas_call x1, Pallas kernels, exchange(): pl.pallas_call(kernel, out_shape=(jax.ShapeDtypeStruct((64, 256), BF), ja...  87.5 us
    unnamed x4, local copies, waits for them, and re-layouts  6.95 us
    dot_general x2, matrix products, dot(): return lax.dot_general(a, b, dims, preferred_element_type=F32)  4.07 us

profile of v2, /device:TPU:0, one launch (start us, length us, event | category | flops | bytes accessed | tf_op | source)
XLA Modules:
  0.0 99.8 jit_solution(12421701772400002855)
XLA Ops:
  1.3 87.5 %shard_map.102 = (bf16[64,256]{1,0:T(8,128)(2,1)}, bf16[2,64,1024]{2,1,0:T(8,128)(2,1)}, bf16[1024,2048]{1,0:T(8,128)(2,1)}, bf16[2048,1024]{1,0:T(8,128)(2,1)}) custom-call(s32[1,64]{1,0:T(1,128)} %chosen_ref.1, f32[1,64]{1,0:T(1,128)} %gates_ref.1, s32[1]{0:T(128)S(6)} %copy.13.count_ref, bf16[256,1024]{1,0:T(8,128)(2,1)} %tok_hbm.1, ...), custom_call_target="tpu_custom_call" | custom-call | flops 14000000000 | bytes 20971520 | tf_op jit(solution)/shard_map/pallas_call | solution.py:537
  88.8 2.0 %convolution_convert_fusion = bf16[256,1024]{1,0:T(8,128)(2,1)} fusion(bf16[64,256]{1,0:T(8,128)(2,1)} %get-tuple-element.8, bf16[2,64,1024]{2,1,0:T(8,128)(2,1)} %get-tuple-element.9), kind=kOutput, calls=%fused_computation | convolution fusion | flops 33816576 | bytes 688128 | tf_op jit(solution)/shard_map/dot_general | solution.py:38
  90.8 2.0 %convolution_convert_fusion.1 = bf16[256,1024]{1,0:T(8,128)(2,1)} fusion(bf16[64,256]{1,0:T(8,128)(2,1)} %get-tuple-element.8, bf16[2,64,1024]{2,1,0:T(8,128)(2,1)} %get-tuple-element.9), kind=kOutput, calls=%fused_computation.1 | convolution fusion | flops 33816576 | bytes 688128 | tf_op jit(solution)/shard_map/dot_general | solution.py:38
  92.8 0.0 copy-start
  92.8 4.9 %copy.14 = bf16[1024,2048]{1,0:T(8,128)(2,1)} copy(bf16[1024,2048]{1,0:T(8,128)(2,1)} %get-tuple-element.18) | data formatting | bytes 8388608
  97.8 0.0 copy-done
  97.8 2.0 %copy.15 = bf16[2048,1024]{1,0:T(8,128)(2,1)} copy(bf16[2048,1024]{1,0:T(8,128)(2,1)S(1)} %copy-done) | data formatting | bytes 8388608
Async XLA Ops:
  92.8 4.9 %copy-start = (bf16[2048,1024]{1,0:T(8,128)(2,1)S(1)}, bf16[2048,1024]{1,0:T(8,128)(2,1)}, u32[]{:S(2)}) copy-start(bf16[2048,1024]{1,0:T(8,128)(2,1)} %get-tuple-element.19) | copy-start | bytes 12582916

commit v3 on v2

--- a/solution.py
+++ b/solution.py
@@ -487,18 +487,26 @@
             tasks[f"fn{q}_{t}"] = fn(q, far)
             tasks[f"fs{q}_{t}"] = fs(q, far)
 
+    moved = {}
+
     def dwo_tile(j):
         def run():
             here = pl.ds(256 * j, 256)
-            dwo[here, :] = dot(hb[0, :, here], rows[1], TN).astype(BF)
-            local_copy(dwo.at[here], dwo_out.at[here])
+            got = dot(hb[0, :, here], rows[1], TN).astype(BF)
+            if j >= 2:
+                moved["o", j - 2].wait()
+            dwo[j % 2] = got
+            moved["o", j] = local_copy(dwo.at[j % 2], dwo_out.at[here])
         return run
 
     def dwi_tile(j):
         def run():
             here = pl.ds(256 * j, 256)
-            dwi[here, :] = dot(rows[0, :, here], hb[1], TN).astype(BF)
-            local_copy(dwi.at[here], dwi_out.at[here])
+            got = dot(rows[0, :, here], hb[1], TN).astype(BF)
+            if j >= 2:
+                moved["i", j - 2].wait()
+            dwi[j % 2] = got
+            moved["i", j] = local_copy(dwi.at[j % 2], dwi_out.at[here])
         return run
 
     for j in range(8):
@@ -522,14 +530,17 @@
 
     for d in sent:
         d.wait_send()
-    for d in opened[4:]:
-        d.wait()
+    for j in (6, 7):
+        moved["o", j].wait()
+    for j in (2, 3):
+        moved["i", j].wait()
 
 
 def exchange(chosen, gates, counts, tokens, cotangent, w_in, w_out):
     vmem = pl.BlockSpec(memory_space=pltpu.VMEM)
     smem = pl.BlockSpec(memory_space=pltpu.SMEM)
     anywhere = pl.BlockSpec(memory_space=pl.ANY)
+    hbm = pl.BlockSpec(memory_space=pltpu.HBM)
 
     def v(*shape, dtype=BF):
         return pltpu.VMEM(shape, dtype)
@@ -537,12 +548,12 @@
     return pl.pallas_call(
         kernel,
         out_shape=(
-            jax.ShapeDtypeStruct((64, 256), BF),
-            jax.ShapeDtypeStruct((2, 64, 1024), BF),
-            jax.ShapeDtypeStruct((1024, 2048), BF),
-            jax.ShapeDtypeStruct((2048, 1024), BF),
+            pltpu.VMEM((64, 256), BF),
+            pltpu.VMEM((2, 64, 1024), BF),
+            pltpu.VMEM((1024, 2048), BF),
+            pltpu.VMEM((2048, 1024), BF),
         ),
-        in_specs=[vmem, vmem, smem] + [anywhere] * 4,
+        in_specs=[vmem, vmem, smem] + [hbm] * 4,
         out_specs=(vmem, vmem, anywhere, anywhere),
         scratch_shapes=[
             v(256, 1024), v(256, 1024), v(1024, 2048), v(2048, 1024),
@@ -567,13 +578,13 @@
             v(2, 2, 4, 2, 64, 512),
             v(2, 2, 3, 64, 512),
             v(2, 2, 3, 64, 512),
-            v(1024, 2048), v(2048, 1024),
+            v(2, 256, 2048), v(2, 256, 1024),
             pltpu.SemaphoreType.DMA((N_COPIES,)),
             pltpu.SemaphoreType.DMA((N_COPIES,)),
             pltpu.SemaphoreType.DMA((N_LOCAL,)),
         ],
         compiler_params=pltpu.CompilerParams(
-            collective_id=0, has_side_effects=True, vmem_limit_bytes=62 * 2**20
+            collective_id=0, has_side_effects=True, vmem_limit_bytes=54 * 2**20
         ),
         cost_estimate=pl.CostEstimate(
             flops=14 * 10**9, bytes_accessed=20 * 2**20, transcendentals=2**19
@@ -581,15 +592,46 @@
     )(chosen, gates, counts, tokens, cotangent, w_in, w_out)
 
 
+def finish_kernel(
+    pick_ref, slots_ref, dwi_in, dwo_in, mixed_ref, d_tok_ref, dwi_out, dwo_out, sem
+):
+    moves = []
+    for src, dst, n in ((dwi_in, dwi_out, 256), (dwo_in, dwo_out, 512)):
+        for j in range(4):
+            here = pl.ds(n * j, n)
+            d = pltpu.make_async_copy(src.at[here], dst.at[here], sem.at[len(moves)])
+            d.start()
+            moves.append(d)
+    mixed_ref[...] = dot(pick_ref[...], slots_ref[0], TN).astype(BF)
+    d_tok_ref[...] = dot(pick_ref[...], slots_ref[1], TN).astype(BF)
+    for d in moves:
+        d.wait()
+
+
+def finish(pick, slots, d_w_in, d_w_out):
+    vmem = pl.BlockSpec(memory_space=pltpu.VMEM)
+    anywhere = pl.BlockSpec(memory_space=pl.ANY)
+    hbm = pl.BlockSpec(memory_space=pltpu.HBM)
+    return pl.pallas_call(
+        finish_kernel,
+        out_shape=(
+            jax.ShapeDtypeStruct((256, 1024), BF),
+            jax.ShapeDtypeStruct((256, 1024), BF),
+            jax.ShapeDtypeStruct((1024, 2048), BF),
+            jax.ShapeDtypeStruct((2048, 1024), BF),
+        ),
+        in_specs=[vmem, vmem, anywhere, anywhere],
+        out_specs=(vmem, vmem, hbm, hbm),
+        scratch_shapes=[pltpu.SemaphoreType.DMA((8,))],
+        compiler_params=pltpu.CompilerParams(vmem_limit_bytes=8 * 2**20),
+        cost_estimate=pl.CostEstimate(
+            flops=6 * 10**7, bytes_accessed=18 * 2**20, transcendentals=0
+        ),
+    )(pick, slots, d_w_in, d_w_out)
+
+
 def local(tokens, w_in, w_out, chosen, counts, gates, cotangent):
-    pick, slots, d_w_in, d_w_out = exchange(
-        chosen, gates, counts, tokens, cotangent, w_in, w_out
-    )
-
-    def scatter(rows):
-        return dot(pick, rows, TN).astype(BF)
-
-    return scatter(slots[0]), scatter(slots[1]), d_w_in, d_w_out
+    return finish(*exchange(chosen, gates, counts, tokens, cotangent, w_in, w_out))
 
 
 def solution(mesh):

time: 100 us -> 92.5 us (0.925)
  local copies, waits for them, and re-layouts: 6.95 us -> 0 us
  matrix products: 4.07 us -> 0 us
  Pallas kernels: 87.5 us -> 91 us
    unnamed x4 -> x0, local copies, waits for them, and re-layouts: 6.95 us -> none
    dot_general x2 -> x0, matrix products: 4.07 us -> none  [dot(): return lax.dot_general(a, b, dims, preferred_element_type=F32)]
    pallas_call x1 -> x2, Pallas kernels: 87.5 us -> 91 us  [the longest x1 86.6 us: exchange(): pl.pallas_call(kernel, out_shape=(pltpu.VMEM((64, 256), BF), pltpu.VMEM((...]
where the time goes in v3:
time: 92.5 us; the launch traced here: 92.4 us
  Pallas kernels  91 us (98%)
  between operations  1.45 us (2%)
    pallas_call x1, Pallas kernels, exchange(): pl.pallas_call(kernel, out_shape=(pltpu.VMEM((64, 256), BF), pltpu.VMEM((...  86.6 us
    pallas_call x1, Pallas kernels, finish(): pl.pallas_call(finish_kernel, out_shape=(jax.ShapeDtypeStruct((256, 1024)...  4.34 us

profile of v3, /device:TPU:0, one launch (start us, length us, event | category | flops | bytes accessed | tf_op | source)
XLA Modules:
  0.0 92.4 jit_solution(12991369213121840068)
XLA Ops:
  1.3 86.6 %shard_map.102 = (bf16[64,256]{1,0:T(8,128)(2,1)S(1)}, bf16[2,64,1024]{2,1,0:T(8,128)(2,1)S(1)}, bf16[1024,2048]{1,0:T(8,128)(2,1)S(1)}, bf16[2048,1024]{1,0:T(8,128)(2,1)S(1)}) custom-call(s32[1,64]{1,0:T(1,128)} %chosen_ref.1, f32[1,64]{1,0:T(1,128)} %gates_ref.1, s32[1]{0:T(128)S(6)} %copy.11.count_ref, bf16[256,1024]{1,0:T(8,128)(2,1)} %tok_hbm.1, ...), custom_call_target="tpu_custom_call" | custom-call | flops 14000000000 | bytes 20971520 | tf_op jit(solution)/shard_map/pallas_call | solution.py:548
  87.9 4.3 %shard_map.103 = (bf16[256,1024]{1,0:T(8,128)(2,1)}, bf16[256,1024]{1,0:T(8,128)(2,1)}, bf16[1024,2048]{1,0:T(8,128)(2,1)}, bf16[2048,1024]{1,0:T(8,128)(2,1)}) custom-call(bf16[64,256]{1,0:T(8,128)(2,1)S(1)} %get-tuple-element.8.pick_ref, bf16[2,64,1024]{2,1,0:T(8,128)(2,1)S(1)} %get-tuple-element.9.slots_ref, ...), custom_call_target="tpu_custom_call" | custom-call | flops 60000000 | bytes 18874368 | tf_op jit(solution)/shard_map/pallas_call | solution.py:615

commit v4 on v3

--- a/solution.py
+++ b/solution.py
@@ -12,21 +12,26 @@
 BF = jnp.bfloat16
 F32 = jnp.float32
 
-N_COPIES = 200
+N_COPIES = 300
 N_LOCAL = 24
 
+CHUNKS = ([(0, 128), (128, 128), (256, 128), (384, 128)], [(0, 256), (256, 256)])
+PHASES = ([(0, 1), (1, 1), (2, 1), (3, 1)], [(0, 2), (2, 2)])
+
 ORDER = (
-    "pick0", "ag1_00", "ag1_01", "pick1", "ag1_10", "meta1", "ag2_00", "ag2_01", "meta2",
-    "ag3_00", "ag3_01", "ag1_11", "ag2_10", "meta", "buildc", "ag4_00", "cmp_00", "ma_00",
-    "ag4_01", "mb_00", "cmp_01", "ma_01", "mc_00", "mb_01", "md_00", "nb_00", "ag3_10", "mc_01",
-    "buildct", "ag2_11", "md_01", "nb_01", "fin_00", "ag3_11", "fin_01", "ag4_10", "cmp_10",
-    "ma_10", "ag4_11", "cmp_11", "fwd_00", "ma_11", "mb_10", "mc_10", "mb_11", "mc_11", "fwd_01",
-    "opp_00", "md_11", "md_10", "nb_10", "ct_00", "opp_01", "nb_11", "ct_01", "fin_10", "e0_0",
-    "e1_0", "fin_11", "dwo0", "fn0_0", "fn1_0", "fwd_10", "e2_0", "dwo1", "fn2_0", "dwo2",
-    "fn3_0", "fs0_0", "fwd_11", "fs1_0", "opp_10", "ct1_11", "fs2_0", "opp_11", "ct_10", "ct2_11",
-    "e0_1", "e1_1", "fs3_0", "dwi0", "dwo3", "fn0_1", "dwo4", "fn1_1", "g3_0", "fn2_1", "dwo5",
-    "dwo6", "fn3_1", "dwi1", "dwi2", "e2_1", "fs0_1", "fs1_1", "fs2_1", "fs3_1", "dwo7", "dwi3",
-    "g3_1",
+    "pick0", "ag1_00", "meta1", "ag1_01", "ag1_02", "ag1_03", "meta2", "ag2_01", "ag2_00", "meta",
+    "ag3_01", "buildct", "ag2_02", "ag2_03", "buildc0", "buildc1", "pick1", "ag1_10", "ag3_00",
+    "ag4_01", "ag4_00", "cmp_01", "ma_01", "cmp_00", "ma_00", "mb_01", "ag3_02", "mc_01", "mb_00",
+    "ag3_03", "mc_00", "md_01", "ag1_11", "md_00", "nb_01", "ag2_10", "ag4_02", "cmp_02", "ma_02",
+    "nb_00", "ag4_03", "cmp_03", "ma_03", "mb_02", "mc_02", "mb_03", "ag2_11", "fin_01", "md_02",
+    "mc_03", "fin_00", "nb_02", "ag3_10", "md_03", "nb_03", "fwd_00", "ag3_11", "fwd_01",
+    "ag4_10", "cmp_10", "fin_02", "ma_10", "fin_03", "mb_10", "ag4_11", "cmp_11", "ma_11",
+    "mc_10", "fwd_02", "opp_00", "mb_11", "mc_11", "opp_01", "fwd_03", "md_10", "nb_10", "md_11",
+    "opp_02", "ct_00", "opp_03", "nb_11", "ct_01", "fin_10", "e0_m", "dwo0", "e1_m", "fin_11",
+    "fn0_m", "fn1_m", "dwo1", "fwd_10", "fn2_m", "e2_m", "dwo2", "dwo3", "fwd_11", "fn3_m",
+    "fs0_m", "fs1_m", "opp_10", "ct1_11", "fs2_m", "opp_11", "ct_10", "ct2_11", "e0_d1", "e1_d1",
+    "dwo4", "dwi0", "fn0_d1", "fn1_d1", "fn2_d1", "dwo5", "dwi1", "e2_d1", "fn3_d1", "fs0_d1",
+    "fs3_m", "dwo6", "fs1_d1", "dwi2", "fs2_d1", "fs3_d1", "dwi3", "g3_m", "dwo7", "g3_d1",
 )
 
 NN = (((1,), (0,)), ((), ()))
@@ -51,7 +56,7 @@
 def kernel(
     chosen_ref, gates_ref, count_ref, tok_hbm, cot_hbm, wi_hbm, wo_hbm,
     pick_out, slots_out, dwi_out, dwo_out,
-    tok, cot, wi, wo, gate, ag, cnt, c_mat, ct, rows, xs, xr, ps, opp_rx, nbr_rx, acc, slope, hb,
+    tok, cot, wi, wo, gate, ag, cnt, c_low, c_high, ct, rows, xs, xr, ps, opp_rx, nbr_rx, acc, slope, hb,
     sub, part, spread, home, f_opp, f_nbr, grouped, s_rx, dwi, dwo,
     send_sem, recv_sem, local_sem,
 ):
@@ -121,11 +126,11 @@
         place = jnp.broadcast_to(column(chosen_ref[...]), (64, 256)).astype(jnp.int32)
         spot = lax.broadcasted_iota(jnp.int32, (64, 256), 1)
         slot = lax.broadcasted_iota(jnp.int32, (64, 256), 0)
-        held = jnp.broadcast_to(count_ref[0], (64, 256))
+        held = jnp.broadcast_to(count_ref[...], (64, 256))
         hit = jnp.where(place == spot, 1.0, 0.0) * jnp.where(slot < held, 1.0, 0.0)
         pick_out[...] = hit.astype(BF)
         gate[...] = jnp.broadcast_to(column(gates_ref[...]), (64, 128))
-        cnt[x, z] = jnp.broadcast_to(count_ref[0], (8, 128))
+        cnt[x, z] = jnp.broadcast_to(count_ref[...], (8, 128))
         load["tok"].wait()
         keep(0, dot(pick_out[...], tok[...]).astype(BF))
 
@@ -134,24 +139,26 @@
         keep(1, (gate[:, 0:1] * dot(pick_out[...], cot[...])).astype(BF))
 
     def keep(t, got):
-        for ph in range(2):
-            for h in range(2):
-                ag[t, ph, h, x, z] = got[32 * ph:32 * ph + 32, 512 * h:512 * h + 512]
+        for b in range(4):
+            for h in range(2):
+                ag[t, h, b, x, z] = got[16 * b:16 * b + 16, 512 * h:512 * h + 512]
 
     tasks["pick0"], tasks["pick1"] = pick0, pick1
 
     def axes(h):
         return (x, z, dev_x, dev_z) if h == 0 else (z, x, dev_z, dev_x)
 
-    def add_gather(t, ph):
-        base = [fresh(7), fresh(7)]
+    def add_gather(t, ph, b0, nb):
+        base = [fresh(8), fresh(8)]
+        blocks = pl.ds(b0, nb)
+        direct = (t, ph) == (0, 0)
 
         def blk(h, fi, si):
-            return ag.at[(t, ph, h) + ((fi, si) if h == 0 else (si, fi))]
+            return ag.at[(t, h, blocks) + ((fi, si) if h == 0 else (si, fi))]
 
         def grp(h, si, first, n):
             many = pl.ds(first, n)
-            return ag.at[(t, ph, h) + ((many, si) if h == 0 else (si, many))]
+            return ag.at[(t, h, blocks) + ((many, si) if h == 0 else (si, many))]
 
         def ag1():
             for h in range(2):
@@ -164,22 +171,24 @@
                 f, s, fd, sd = axes(h)
                 for n, d in three:
                     recv(base[h] + n, blk(h, wrap(f - d), s), fd[d])
-                for n, d in both:
+                for n, d in three if direct else both:
                     send(base[h] + 3 + n, grp(h, s, 0, 4), grp(h, s, 0, 4), sd[d])
 
         def ag3():
+            for h in range(2):
+                f, s, fd, sd = axes(h)
+                for n, d in three if direct else both:
+                    recv(base[h] + 3 + n, grp(h, wrap(s - d), 0, 4), sd[d])
+                    if not direct:
+                        g = grp(h, wrap(s - d), 2 * n, 2)
+                        send(base[h] + 6 + n, g, g, sd[d])
+
+        def ag4():
             for h in range(2):
                 f, s, fd, sd = axes(h)
                 for n, d in both:
-                    recv(base[h] + 3 + n, grp(h, wrap(s - d), 0, 4), sd[d])
-                    g = grp(h, wrap(s - d), 2 * n, 2)
-                    send(base[h] + 5 + n, g, g, sd[d])
-
-        def ag4():
-            for h in range(2):
-                f, s, fd, sd = axes(h)
-                for n, d in both:
-                    recv(base[h] + 5 + n, grp(h, wrap(s + 2), 2 * n, 2), sd[d])
+                    if not direct:
+                        recv(base[h] + 6 + n, grp(h, wrap(s + 2), 2 * n, 2), sd[d])
 
         for name, f in (("ag1", ag1), ("ag2", ag2), ("ag3", ag3), ("ag4", ag4)):
             tasks[f"{name}_{t}{ph}"] = f
@@ -202,73 +211,78 @@
 
     tasks.update(meta1=meta1, meta2=meta2, meta=meta)
 
-    def places():
-        first, second = [], []
+    def places(upto):
         total = jnp.zeros((8, 128), jnp.int32)
+        found = []
+        for b in range(upto):
+            found.append([])
+            for i in range(16):
+                held = jnp.clip(cnt[i // 4, i % 4] - 16 * b, 0, 16)
+                found[b].append((total, held))
+                total = total + held
+        return found
+
+    def build_c(out, blocks, first_row):
+        found = places(blocks[-1] + 1)
+        lane = lax.broadcasted_iota(jnp.int32, (8, 128), 1)
+        part_of, slot = lane // 16, lane % 16
+        row = lax.broadcasted_iota(jnp.int32, (256, 128), 0) + first_row
+        for b in blocks:
+            for j in range(2):
+                start, held = found[b][8 * j]
+                for i in range(1, 8):
+                    start = jnp.where(part_of == i, found[b][8 * j + i][0], start)
+                    held = jnp.where(part_of == i, found[b][8 * j + i][1], held)
+                place = jnp.where(slot < held, start + slot, -1)
+                hit = jnp.broadcast_to(place[0:1], (256, 128)) == row
+                at = 256 * (b - blocks[0]) + 128 * j
+                out[:, at:at + 128] = jnp.where(hit, 1.0, 0.0).astype(BF)
+
+    def buildc0():
+        build_c(c_low, (0, 1), 0)
+
+    def buildc1():
+        build_c(c_high, (1, 2, 3), 256)
+
+    def buildct():
+        found = places(4)
+        slot = lax.broadcasted_iota(jnp.int32, (16, 128), 0)
+        lane = lax.broadcasted_iota(jnp.int32, (16, 128), 1)
         for i in range(16):
-            held = jnp.minimum(cnt[i // 4, i % 4], 32)
-            first.append((total, held))
-            total = total + held
-        for i in range(16):
-            held = jnp.maximum(cnt[i // 4, i % 4] - 32, 0)
-            second.append((total, held))
-            total = total + held
-        return first, second
-
-    def lane_places(shards):
-        lane = lax.broadcasted_iota(jnp.int32, (8, 128), 1)
-        quarter, slot = lane // 32, lane % 32
-        tiles = []
-        for b in range(4):
-            start, held = shards[4 * b + 3]
-            for j in (2, 1, 0):
-                start = jnp.where(quarter == j, shards[4 * b + j][0], start)
-                held = jnp.where(quarter == j, shards[4 * b + j][1], held)
-            tiles.append(jnp.where(slot < held, start + slot, -1))
-        return tiles
-
-    def buildc():
-        first, second = places()
-        row = lax.broadcasted_iota(jnp.int32, (256, 128), 0)
-        for n, (shards, k) in enumerate(((first, 0), (first, 1), (second, 1))):
-            for b, tile in enumerate(lane_places(shards)):
-                hit = jnp.broadcast_to(tile[0:1], (256, 128)) == row + 256 * k
-                c_mat[n, :, 128 * b:128 * b + 128] = jnp.where(hit, 1.0, 0.0).astype(BF)
-
-    def buildct():
-        first, second = places()
-        slot = lax.broadcasted_iota(jnp.int32, (32, 128), 0)
-        lane = lax.broadcasted_iota(jnp.int32, (32, 128), 1)
-        for i in range(16):
-            for ph, shards in ((0, first), (1, second)):
-                start = jnp.broadcast_to(shards[i][0][0:1], (32, 128))
-                held = jnp.broadcast_to(shards[i][1][0:1], (32, 128))
+            for b in range(4):
+                start = jnp.broadcast_to(found[b][i][0][0:1], (16, 128))
+                held = jnp.broadcast_to(found[b][i][1][0:1], (16, 128))
                 place = jnp.where(slot < held, start + slot, -1)
-                for b in range(4):
-                    hit = place == lane + 128 * b
-                    ct[i // 4, i % 4, 32 * ph:32 * ph + 32, 128 * b:128 * b + 128] = jnp.where(
+                for j in range(4):
+                    hit = place == lane + 128 * j
+                    ct[i // 4, i % 4, 16 * b:16 * b + 16, 128 * j:128 * j + 128] = jnp.where(
                         hit, 1.0, 0.0
                     ).astype(BF)
 
-    tasks["buildc"], tasks["buildct"] = buildc, buildct
+    tasks.update(buildc0=buildc0, buildc1=buildc1, buildct=buildct)
 
     def hidden_cols(core, yy, width=256):
         return pl.ds(pl.multiple_of(core * 1024 + yy * width, width), width)
 
-    def add_chunk(t, k):
-        mine = pl.ds(256 * k, 256)
+    loaded = set()
+    incoming = {}
+
+    def add_chunk(t, k, r0, nr):
+        mine = pl.ds(r0, nr)
+        hr = nr // 2
         ic, io, inb = fresh(2), fresh(2), fresh(2)
         iy, iw, ih = fresh(2), fresh(2), fresh(4)
         far = lax.div(wrap(y + 2), 2)
         near = 1 - far
 
         def cmp():
-            for h in range(2):
-                cols = slice(512 * h, 512 * h + 512)
-                got = dot(c_mat[k], ag[t, 0, h].reshape(512, 512))
-                if k == 1:
-                    got += dot(c_mat[2], ag[t, 1, h].reshape(512, 512))
-                rows[t, mine, cols] = got.astype(BF)
+            b0, b1 = (0 if r0 < 256 else 1), (r0 + nr) // 128
+            width = 256 * (b1 - b0)
+            at = r0 % 256
+            picks = (c_low if r0 < 256 else c_high)[at:at + nr, :width]
+            for h in range(2):
+                got = dot(picks, ag[t, h, b0:b1].reshape(width, 512))
+                rows[t, mine, 512 * h:512 * h + 512] = got.astype(BF)
 
         def pair(core, p):
             left = rows[t, mine, :]
@@ -278,29 +292,37 @@
 
         def for_other(p, n):
             got = pair(oc, p).astype(BF)
-            xs[t, k, p, 0] = got[:, :256]
-            xs[t, k, p, 1] = got[:, 256:]
-            send(ic + n, xs.at[t, k, p], xr.at[t, k, p], dev_c)
+            xs[t, p, 0, mine] = got[:, :256]
+            xs[t, p, 1, mine] = got[:, 256:]
+            tiles = pl.ds(0, 2)
+            send(ic + n, xs.at[t, p, tiles, mine], xr.at[t, p, tiles, mine], dev_c)
 
         def for_self(p, n):
             got = pair(c, p)
-            recv(ic + n, xr.at[t, k, p], dev_c)
-            acc[t, k, p, 0] = got[:, :256] + xr[t, k, p, 0].astype(F32)
-            acc[t, k, p, 1] = got[:, 256:] + xr[t, k, p, 1].astype(F32)
+            recv(ic + n, xr.at[t, p, pl.ds(0, 2), mine], dev_c)
+            acc[t, p, 0, mine] = got[:, :256] + xr[t, p, 0, mine].astype(F32)
+            acc[t, p, 1, mine] = got[:, 256:] + xr[t, p, 1, mine].astype(F32)
 
         def tile(yy):
-            return (t, k, lax.div(yy, 2), lax.rem(yy, 2))
+            return (t, lax.div(yy, 2), lax.rem(yy, 2), mine)
 
         def ma():
-            if k == 0:
+            if t not in loaded:
+                loaded.add(t)
                 load[t].wait()
             for_other(far, 0)
 
+        def opp_landing(n):
+            return (t, n, pl.ds(r0 // 2, hr))
+
         def mb():
             for_self(far, 0)
-            ps[t, k, 0] = acc[tile(wrap(y + 2))].astype(BF)
+            ps[t, 0, mine] = acc[tile(wrap(y + 2))].astype(BF)
             for n, d in both:
-                send(io + n, ps.at[t, k, 0, pl.ds(128 * n, 128)], opp_rx.at[t, k, n], dev_y[d])
+                send(
+                    io + n, ps.at[t, 0, pl.ds(r0 + hr * n, hr)], opp_rx.at[opp_landing(n)],
+                    dev_y[d],
+                )
 
         def mc():
             for_other(near, 1)
@@ -310,29 +332,30 @@
 
         def nb():
             for n, d in both:
-                recv(io + n, opp_rx.at[t, k, n], dev_y[d])
+                recv(io + n, opp_rx.at[opp_landing(n)], dev_y[d])
                 got = acc[tile(wrap(y + d))]
-                here = slice(128 * n, 128 * n + 128)
-                away = slice(128 - 128 * n, 256 - 128 * n)
-                ps[t, k, 1 + n, here] = (got[here] + opp_rx[t, k, n].astype(F32)).astype(BF)
-                ps[t, k, 1 + n, away] = got[away].astype(BF)
-                send(inb + n, ps.at[t, k, 1 + n], nbr_rx.at[t, k, n], dev_y[d])
+                here = slice(hr * n, hr * n + hr)
+                away = slice(hr - hr * n, nr - hr * n)
+                added = got[here] + opp_rx[opp_landing(n)].astype(F32)
+                ps[t, 1 + n, pl.ds(r0 + here.start, hr)] = added.astype(BF)
+                ps[t, 1 + n, pl.ds(r0 + away.start, hr)] = got[away].astype(BF)
+                send(inb + n, ps.at[t, 1 + n, mine], nbr_rx.at[t, n, mine], dev_y[d])
 
         def piece(core, yy):
             return hb.at[t, mine, hidden_cols(core, yy)]
 
         def half(yy, n):
-            return hb.at[t, pl.ds(256 * k + 128 * n, 128), hidden_cols(c, yy)]
+            return hb.at[t, pl.ds(r0 + hr * n, hr), hidden_cols(c, yy)]
 
         def fin():
             for n, d in both:
-                recv(inb + n, nbr_rx.at[t, k, n], dev_y[d])
-            total = acc[tile(y)] + nbr_rx[t, k, 0].astype(F32) + nbr_rx[t, k, 1].astype(F32)
+                recv(inb + n, nbr_rx.at[t, n, mine], dev_y[d])
+            total = acc[tile(y)] + nbr_rx[t, 0, mine].astype(F32) + nbr_rx[t, 1, mine].astype(F32)
             if t == 0:
                 total, slopes = gelu_pair(total)
-                slope[k] = slopes
+                slope[mine] = slopes
             else:
-                total = total * slope[k]
+                total = total * slope[mine]
             hb[t, mine, hidden_cols(c, y)] = total.astype(BF)
             p = piece(c, y)
             send(iy, p, p, dev_y[1])
@@ -359,18 +382,27 @@
         def far_in():
             recv(ih + 3, piece(oc, wrap(y + 2)), dev_c)
 
+        incoming.setdefault((t, r0 // 256), []).append((near_in, far_in))
+        for f in (cmp, ma, mb, mc, md, nb, fin, fwd, opp):
+            tasks[f"{f.__name__}_{t}{k}"] = f
+
+    def add_contract(t, half):
+        mine = pl.ds(256 * half, 256)
+        arrivals = incoming[t, half]
+
         def whole():
-            near_in()
-            far_in()
+            for near_in, far_in in arrivals:
+                near_in()
+                far_in()
 
             def step(n, carry):
-                cols = pl.ds(pl.multiple_of(n * 256, 256), 256)
+                cols = pl.ds(pl.multiple_of(n * 512, 512), 512)
                 left = hb[t, mine, :]
                 got = dot(left, wo[:, cols]) if t == 0 else dot(left, wi[cols, :], NT)
                 part[t, mine, cols] = got.astype(BF)
                 return carry
 
-            lax.fori_loop(0, 4, step, 0)
+            lax.fori_loop(0, 2, step, 0)
 
         def product(core, yy):
             units = hidden_cols(core, yy)
@@ -378,30 +410,32 @@
             return dot(left, wo[units, :]) if t == 0 else dot(left, wi[:, units], NT)
 
         def ct1():
-            near_in()
+            for near_in, far_in in arrivals[:-1]:
+                near_in()
+                far_in()
+            arrivals[-1][0]()
             sub[...] = product(c, y)
 
             def step(n, carry):
-                sub[...] += product(lax.rem(c + lax.div(n, 3), 2), wrap(y + 3 + lax.rem(n, 3)))
+                core = lax.rem(c + lax.div(n + 2, 4), 2)
+                away = lax.div(n + 2, 4) * (n + 1) + (1 - lax.div(n + 2, 4)) * (2 * n + 3)
+                sub[...] += product(core, wrap(y + away))
                 return carry
 
-            lax.fori_loop(0, 1, lambda n, carry: step(2, carry), 0)
-            lax.fori_loop(3, 6, step, 0)
-            lax.fori_loop(0, 1, step, 0)
+            lax.fori_loop(0, 5, step, 0)
 
         def ct2():
-            far_in()
+            arrivals[-1][1]()
             got = sub[...] + product(c, wrap(y + 2)) + product(oc, wrap(y + 2))
             part[t, mine, :] = got.astype(BF)
 
-        for f in (cmp, ma, mb, mc, md, nb, fin, fwd, opp):
-            tasks[f"{f.__name__}_{t}{k}"] = f
-        if (t, k) == (1, 1):
+        if (t, half) == (1, 1):
             tasks["ct1_11"], tasks["ct2_11"] = ct1, ct2
         else:
-            tasks[f"ct_{t}{k}"] = whole
+            tasks[f"ct_{t}{half}"] = whole
 
     def add_home(t):
+        tag = ("m", "d1")[t]
         base = [fresh(19), fresh(19)]
 
         def group(h, fi):
@@ -482,10 +516,10 @@
                 slots_out[t, :, 512 * h:512 * h + 512] = got.astype(BF)
 
         for f in (e0, e1, e2, g3):
-            tasks[f"{f.__name__}_{t}"] = f
+            tasks[f"{f.__name__}_{tag}"] = f
         for q, far in enumerate((2, 1, -1, 0)):
-            tasks[f"fn{q}_{t}"] = fn(q, far)
-            tasks[f"fs{q}_{t}"] = fs(q, far)
+            tasks[f"fn{q}_{tag}"] = fn(q, far)
+            tasks[f"fs{q}_{tag}"] = fs(q, far)
 
     moved = {}
 
@@ -514,9 +548,12 @@
     for j in range(4):
         tasks[f"dwi{j}"] = dwi_tile(j)
     for t in range(2):
-        for i in range(2):
-            add_gather(t, i)
-            add_chunk(t, i)
+        for ph, (b0, nb) in enumerate(PHASES[t]):
+            add_gather(t, ph, b0, nb)
+        for k, (r0, nr) in enumerate(CHUNKS[t]):
+            add_chunk(t, k, r0, nr)
+        for half in range(2):
+            add_contract(t, half)
         add_home(t)
 
     entered = False
@@ -538,7 +575,6 @@
 
 def exchange(chosen, gates, counts, tokens, cotangent, w_in, w_out):
     vmem = pl.BlockSpec(memory_space=pltpu.VMEM)
-    smem = pl.BlockSpec(memory_space=pltpu.SMEM)
     anywhere = pl.BlockSpec(memory_space=pl.ANY)
     hbm = pl.BlockSpec(memory_space=pltpu.HBM)
 
@@ -553,22 +589,22 @@
             pltpu.VMEM((1024, 2048), BF),
             pltpu.VMEM((2048, 1024), BF),
         ),
-        in_specs=[vmem, vmem, smem] + [hbm] * 4,
+        in_specs=[vmem] * 3 + [hbm] * 4,
         out_specs=(vmem, vmem, anywhere, anywhere),
         scratch_shapes=[
             v(256, 1024), v(256, 1024), v(1024, 2048), v(2048, 1024),
             v(64, 128, dtype=F32),
-            v(2, 2, 2, 4, 4, 32, 512),
+            v(2, 2, 4, 4, 4, 16, 512),
             v(4, 4, 8, 128, dtype=jnp.int32),
-            v(3, 256, 512),
+            v(256, 512), v(256, 768),
             v(4, 4, 64, 512),
             v(2, 512, 1024),
-            v(2, 2, 2, 2, 256, 256), v(2, 2, 2, 2, 256, 256),
-            v(2, 2, 3, 256, 256),
-            v(2, 2, 2, 128, 256),
-            v(2, 2, 2, 256, 256),
-            v(2, 2, 2, 2, 256, 256, dtype=F32),
-            v(2, 256, 256, dtype=F32),
+            v(2, 2, 2, 512, 256), v(2, 2, 2, 512, 256),
+            v(2, 3, 512, 256),
+            v(2, 2, 256, 256),
+            v(2, 2, 512, 256),
+            v(2, 2, 2, 512, 256, dtype=F32),
+            v(512, 256, dtype=F32),
             v(2, 512, 2048),
             v(256, 1024, dtype=F32),
             v(2, 512, 1024),
@@ -631,7 +667,7 @@
 
 
 def local(tokens, w_in, w_out, chosen, counts, gates, cotangent):
-    return finish(*exchange(chosen, gates, counts, tokens, cotangent, w_in, w_out))
+    return finish(*exchange(chosen, gates, counts.reshape(1, 1), tokens, cotangent, w_in, w_out))
 
 
 def solution(mesh):

time: 92.5 us -> 91.5 us (0.989)
  Pallas kernels: 91 us -> 89.9 us
    pallas_call x1, Pallas kernels: 86.6 us -> 85.6 us  [exchange(): pl.pallas_call(kernel, out_shape=(pltpu.VMEM((64, 256), BF), pltpu.VMEM((...]
where the time goes in v4:
time: 91.5 us; the launch traced here: 91.4 us
  Pallas kernels  89.9 us (98%)
  between operations  1.45 us (2%)
    pallas_call x1, Pallas kernels, exchange(): pl.pallas_call(kernel, out_shape=(pltpu.VMEM((64, 256), BF), pltpu.VMEM((...  85.6 us
    pallas_call x1, Pallas kernels, finish(): pl.pallas_call(finish_kernel, out_shape=(jax.ShapeDtypeStruct((256, 1024)...  4.34 us

profile of v4, /device:TPU:0, one launch (start us, length us, event | category | flops | bytes accessed | tf_op | source)
XLA Modules:
  0.0 91.4 jit_solution(2826112216301575334)
XLA Ops:
  1.3 85.6 %shard_map.102 = (bf16[64,256]{1,0:T(8,128)(2,1)S(1)}, bf16[2,64,1024]{2,1,0:T(8,128)(2,1)S(1)}, bf16[1024,2048]{1,0:T(8,128)(2,1)S(1)}, bf16[2048,1024]{1,0:T(8,128)(2,1)S(1)}) custom-call(s32[1,64]{1,0:T(1,128)} %chosen_ref.1, f32[1,64]{1,0:T(1,128)} %gates_ref.1, s32[1,1]{1,0:T(1,128)} %bitcast.1.count_ref, bf16[256,1024]{1,0:T(8,128)(2,1)} %tok_hbm.1, ...), custom_call_target="tpu_custom_call" | custom-call | flops 14000000000 | bytes 20971520 | tf_op jit(solution)/shard_map/pallas_call | solution.py:584
  86.9 4.3 %shard_map.103 = (bf16[256,1024]{1,0:T(8,128)(2,1)}, bf16[256,1024]{1,0:T(8,128)(2,1)}, bf16[1024,2048]{1,0:T(8,128)(2,1)}, bf16[2048,1024]{1,0:T(8,128)(2,1)}) custom-call(bf16[64,256]{1,0:T(8,128)(2,1)S(1)} %get-tuple-element.8.pick_ref, bf16[2,64,1024]{2,1,0:T(8,128)(2,1)S(1)} %get-tuple-element.9.slots_ref, ...), custom_call_target="tpu_custom_call" | custom-call | flops 60000000 | bytes 18874368 | tf_op jit(solution)/shard_map/pallas_call | solution.py:651

commit v5 on v4

--- a/solution.py
+++ b/solution.py
@@ -12,26 +12,29 @@
 BF = jnp.bfloat16
 F32 = jnp.float32
 
-N_COPIES = 300
+N_COPIES = 345
 N_LOCAL = 24
 
 CHUNKS = ([(0, 128), (128, 128), (256, 128), (384, 128)], [(0, 256), (256, 256)])
 PHASES = ([(0, 1), (1, 1), (2, 1), (3, 1)], [(0, 2), (2, 2)])
+HOMES = (('m', 0, 0, 512, 0, 64), ('d1', 1, 0, 512, 0, 64))
+HOME_SLOTS = 128
 
 ORDER = (
-    "pick0", "ag1_00", "meta1", "ag1_01", "ag1_02", "ag1_03", "meta2", "ag2_01", "ag2_00", "meta",
-    "ag3_01", "buildct", "ag2_02", "ag2_03", "buildc0", "buildc1", "pick1", "ag1_10", "ag3_00",
-    "ag4_01", "ag4_00", "cmp_01", "ma_01", "cmp_00", "ma_00", "mb_01", "ag3_02", "mc_01", "mb_00",
-    "ag3_03", "mc_00", "md_01", "ag1_11", "md_00", "nb_01", "ag2_10", "ag4_02", "cmp_02", "ma_02",
-    "nb_00", "ag4_03", "cmp_03", "ma_03", "mb_02", "mc_02", "mb_03", "ag2_11", "fin_01", "md_02",
-    "mc_03", "fin_00", "nb_02", "ag3_10", "md_03", "nb_03", "fwd_00", "ag3_11", "fwd_01",
-    "ag4_10", "cmp_10", "fin_02", "ma_10", "fin_03", "mb_10", "ag4_11", "cmp_11", "ma_11",
-    "mc_10", "fwd_02", "opp_00", "mb_11", "mc_11", "opp_01", "fwd_03", "md_10", "nb_10", "md_11",
-    "opp_02", "ct_00", "opp_03", "nb_11", "ct_01", "fin_10", "e0_m", "dwo0", "e1_m", "fin_11",
-    "fn0_m", "fn1_m", "dwo1", "fwd_10", "fn2_m", "e2_m", "dwo2", "dwo3", "fwd_11", "fn3_m",
-    "fs0_m", "fs1_m", "opp_10", "ct1_11", "fs2_m", "opp_11", "ct_10", "ct2_11", "e0_d1", "e1_d1",
-    "dwo4", "dwi0", "fn0_d1", "fn1_d1", "fn2_d1", "dwo5", "dwi1", "e2_d1", "fn3_d1", "fs0_d1",
-    "fs3_m", "dwo6", "fs1_d1", "dwi2", "fs2_d1", "fs3_d1", "dwi3", "g3_m", "dwo7", "g3_d1",
+    "pick0", "pick1", "ag1_00", "meta1", "ag1_01", "ag1_02", "ag1_03", "meta2", "ag2_01",
+    "ag2_00", "ag3_01", "meta", "ag2_02", "ag1_10", "ag2_03", "ag1_11", "buildc1", "buildc0",
+    "ag3_00", "ag4_00", "cmp_00", "ag4_01", "cmp_01", "ma_01", "ma_00", "mb_01", "mb_00",
+    "ag3_02", "mc_01", "mc_00", "ag3_03", "ag2_10", "md_01", "nb_01", "md_00", "nb_00", "ag4_02",
+    "cmp_02", "ma_02", "ag2_11", "ag4_03", "cmp_03", "mb_02", "ma_03", "fin_01", "mc_02", "mb_03",
+    "fin_00", "ag3_10", "mc_03", "md_02", "nb_02", "ag3_11", "md_03", "nb_03", "buildct",
+    "fwd_00", "fwd_01", "ag4_10", "cmp_10", "ma_10", "fin_02", "ag4_11", "cmp_11", "fin_03",
+    "ma_11", "mb_10", "mb_11", "mc_10", "fwd_02", "mc_11", "opp_01", "fwd_03", "opp_00", "md_10",
+    "md_11", "nb_10", "ct_00", "opp_02", "nb_11", "opp_03", "ct_01", "fin_10", "e0_m", "fin_11",
+    "e1_m", "fn0_m", "fwd_10", "fn1_m", "fn2_m", "fn3_m", "dwo0", "dwo1", "e2_m", "fwd_11",
+    "dwo2", "fs0_m", "fs1_m", "opp_10", "ct1_11", "fs2_m", "opp_11", "ct_10", "ct2_11", "e0_d1",
+    "e1_d1", "dwo3", "fn0_d1", "fn1_d1", "dwo4", "fn2_d1", "dwi0", "fn3_d1", "dwo5", "dwo6",
+    "dwi1", "e2_d1", "dwo7", "fs0_d1", "dwi2", "fs1_d1", "fs2_d1", "fs3_d1", "fs3_m", "g3_m",
+    "dwi3", "g3_d1",
 )
 
 NN = (((1,), (0,)), ((), ()))
@@ -57,7 +60,7 @@
     chosen_ref, gates_ref, count_ref, tok_hbm, cot_hbm, wi_hbm, wo_hbm,
     pick_out, slots_out, dwi_out, dwo_out,
     tok, cot, wi, wo, gate, ag, cnt, c_low, c_high, ct, rows, xs, xr, ps, opp_rx, nbr_rx, acc, slope, hb,
-    sub, part, spread, home, f_opp, f_nbr, grouped, s_rx, dwi, dwo,
+    sub, part, spread, home, f_opp, f_nbr, grouped, s_rx, early, dwi, dwo,
     send_sem, recv_sem, local_sem,
 ):
     dp, ex = lax.axis_index("dp"), lax.axis_index("expert")
@@ -425,101 +428,120 @@
             lax.fori_loop(0, 5, step, 0)
 
         def ct2():
+            sub[...] += product(c, wrap(y + 2))
             arrivals[-1][1]()
-            got = sub[...] + product(c, wrap(y + 2)) + product(oc, wrap(y + 2))
-            part[t, mine, :] = got.astype(BF)
+            part[t, mine, :] = (sub[...] + product(oc, wrap(y + 2))).astype(BF)
 
         if (t, half) == (1, 1):
             tasks["ct1_11"], tasks["ct2_11"] = ct1, ct2
         else:
             tasks[f"ct_{t}{half}"] = whole
 
-    def add_home(t):
-        tag = ("m", "d1")[t]
+    def add_home(tag, t, r0, nr, s0, ns, at, in_four):
         base = [fresh(19), fresh(19)]
+        mine = pl.ds(at, ns)
+        order = (2, 1, -1, 0)
+
+        def targets(q, s):
+            return pl.ds(wrap(s + order[q]), 1) if in_four else pl.ds(0, 4)
 
         def group(h, fi):
-            picks = ct[fi] if h == 0 else ct[:, fi]
-            got = dot(picks.reshape(256, 512), part[t, :, 512 * h:512 * h + 512])
-            return got.reshape(4, 64, 512)
+            slots, those = slice(s0, s0 + ns), slice(r0, r0 + nr)
+            picks = ct[fi, :, slots, those] if h == 0 else ct[:, fi, slots, those]
+            cols = slice(512 * h, 512 * h + 512)
+            return dot(picks.reshape(4 * ns, nr), part[t, those, cols]).reshape(4, ns, 512)
 
         def e0():
             for h in range(2):
                 f, s, fd, sd = axes(h)
-                spread[t, h, 0] = group(h, wrap(f + 2)).astype(BF)
-                for q, far in enumerate((2, 1, -1, 0)):
-                    to = wrap(s + far)
+                spread[h, 0, :, mine] = group(h, wrap(f + 2)).astype(BF)
+                for q in range(4 if in_four else 1):
+                    to = targets(q, s)
                     for n, d in both:
                         send(
-                            base[h] + 2 * q + n, spread.at[t, h, 0, to, pl.ds(32 * n, 32)],
-                            f_opp.at[t, h, q, n], fd[d],
+                            base[h] + 2 * q + n, spread.at[h, 0, to, mine, pl.ds(256 * n, 256)],
+                            f_opp.at[h, n, to, mine], fd[d],
                         )
 
         def e1():
             for h in range(2):
                 f, s, fd, sd = axes(h)
                 for n, d in both:
-                    spread[t, h, 1 + n] = group(h, wrap(f + d)).astype(BF)
+                    spread[h, 1 + n, :, mine] = group(h, wrap(f + d)).astype(BF)
 
         def e2():
             for h in range(2):
-                home[t, h] = group(h, axes(h)[0])
-
-        def fn(q, far):
+                home[h, :, mine] = group(h, axes(h)[0])
+
+        def fn(q):
             def run():
                 for h in range(2):
                     f, s, fd, sd = axes(h)
-                    to = wrap(s + far)
+                    to = targets(q, s)
                     for n, d in both:
-                        recv(base[h] + 2 * q + n, f_opp.at[t, h, q, n], fd[d])
-                        here = slice(32 * n, 32 * n + 32)
-                        spread[t, h, 1 + n, to, here] = (
-                            spread[t, h, 1 + n, to, here].astype(F32)
-                            + f_opp[t, h, q, n].astype(F32)
+                        recv(base[h] + 2 * q + n, f_opp.at[h, n, to, mine], fd[d])
+                        cols = slice(256 * n, 256 * n + 256)
+                        spread[h, 1 + n, to, mine, cols] = (
+                            spread[h, 1 + n, to, mine, cols].astype(F32)
+                            + f_opp[h, n, to, mine].astype(F32)
                         ).astype(BF)
                         send(
-                            base[h] + 8 + 2 * q + n, spread.at[t, h, 1 + n, to],
-                            f_nbr.at[t, h, q, n], fd[d],
+                            base[h] + 8 + 2 * q + n, spread.at[h, 1 + n, to, mine],
+                            f_nbr.at[h, n, to, mine], fd[d],
                         )
             return run
 
-        def fs(q, far):
+        def fs(q):
             def run():
                 for h in range(2):
                     f, s, fd, sd = axes(h)
-                    to = wrap(s + far)
+                    to = targets(q, s)
                     for n, d in both:
-                        recv(base[h] + 8 + 2 * q + n, f_nbr.at[t, h, q, n], fd[d])
+                        recv(base[h] + 8 + 2 * q + n, f_nbr.at[h, n, to, mine], fd[d])
                     got = (
-                        home[t, h, to]
-                        + f_nbr[t, h, q, 0].astype(F32)
-                        + f_nbr[t, h, q, 1].astype(F32)
+                        home[h, to, mine]
+                        + f_nbr[h, 0, to, mine].astype(F32)
+                        + f_nbr[h, 1, to, mine].astype(F32)
                     )
-                    if q == 3:
-                        home[t, h, to] = got
-                    else:
-                        grouped[t, h, q] = got.astype(BF)
-                        send(
-                            base[h] + 16 + q, grouped.at[t, h, q], s_rx.at[t, h, q], sd[far]
-                        )
+                    home[h, to, mine] = got
+                    grouped[h, to, mine] = got.astype(BF)
+                    for p in (q,) if in_four else range(4):
+                        if p < 3:
+                            away = wrap(s + order[p])
+                            send(
+                                base[h] + 16 + p, grouped.at[h, away, mine],
+                                s_rx.at[h, p, mine], sd[order[p]],
+                            )
             return run
 
         def g3():
             for h in range(2):
                 f, s, fd, sd = axes(h)
-                got = home[t, h, s]
-                for q, far in enumerate((2, 1, -1)):
-                    recv(base[h] + 16 + q, s_rx.at[t, h, q], sd[far])
-                    got = got + s_rx[t, h, q].astype(F32)
-                if t == 0:
-                    got = gate[:, 0:1] * got
-                slots_out[t, :, 512 * h:512 * h + 512] = got.astype(BF)
+                got = home[h, s, mine]
+                for p in range(3):
+                    recv(base[h] + 16 + p, s_rx.at[h, p, mine], sd[order[p]])
+                    got = got + s_rx[h, p, mine].astype(F32)
+                cols = slice(512 * h, 512 * h + 512)
+                if ns == 32:
+                    early[t, :, cols] = got
+                    continue
+                pieces = ((slice(0, 64), got),)
+                if ns == 48:
+                    pieces = (
+                        (slice(0, 16), early[t, 0:16, cols]),
+                        (slice(16, 32), early[t, 16:32, cols] + got[0:16]),
+                        (slice(32, 64), got[16:48]),
+                    )
+                for slots, value in pieces:
+                    if t == 0:
+                        value = gate[slots, 0:1] * value
+                    slots_out[t, slots, cols] = value.astype(BF)
 
         for f in (e0, e1, e2, g3):
             tasks[f"{f.__name__}_{tag}"] = f
-        for q, far in enumerate((2, 1, -1, 0)):
-            tasks[f"fn{q}_{tag}"] = fn(q, far)
-            tasks[f"fs{q}_{tag}"] = fs(q, far)
+        for q in range(4 if in_four else 1):
+            tasks[f"fn{q}_{tag}"] = fn(q)
+            tasks[f"fs{q}_{tag}"] = fs(q)
 
     moved = {}
 
@@ -547,6 +569,10 @@
         tasks[f"dwo{j}"] = dwo_tile(j)
     for j in range(4):
         tasks[f"dwi{j}"] = dwi_tile(j)
+    at = 0
+    for tag, t, r0, nr, s0, ns in HOMES:
+        add_home(tag, t, r0, nr, s0, ns, at, ns == 64 or tag == "d1")
+        at += ns
     for t in range(2):
         for ph, (b0, nb) in enumerate(PHASES[t]):
             add_gather(t, ph, b0, nb)
@@ -554,7 +580,6 @@
             add_chunk(t, k, r0, nr)
         for half in range(2):
             add_contract(t, half)
-        add_home(t)
 
     entered = False
     for name in ORDER:
@@ -608,12 +633,13 @@
             v(2, 512, 2048),
             v(256, 1024, dtype=F32),
             v(2, 512, 1024),
-            v(2, 2, 3, 4, 64, 512),
-            v(2, 2, 4, 64, 512, dtype=F32),
-            v(2, 2, 4, 2, 32, 512),
-            v(2, 2, 4, 2, 64, 512),
-            v(2, 2, 3, 64, 512),
-            v(2, 2, 3, 64, 512),
+            v(2, 3, 4, HOME_SLOTS, 512),
+            v(2, 4, HOME_SLOTS, 512, dtype=F32),
+            v(2, 2, 4, HOME_SLOTS, 256),
+            v(2, 2, 4, HOME_SLOTS, 512),
+            v(2, 4, HOME_SLOTS, 512),
+            v(2, 3, HOME_SLOTS, 512),
+            v(2, 32, 1024, dtype=F32),
             v(2, 256, 2048), v(2, 256, 1024),
             pltpu.SemaphoreType.DMA((N_COPIES,)),
             pltpu.SemaphoreType.DMA((N_COPIES,)),
@@ -629,7 +655,7 @@
 
 
 def finish_kernel(
-    pick_ref, slots_ref, dwi_in, dwo_in, mixed_ref, d_tok_ref, dwi_out, dwo_out, sem
+    pick_ref, slots_ref, dwi_in, dwo_in, mixed_out, d_tok_out, dwi_out, dwo_out, spot, sem
 ):
     moves = []
     for src, dst, n in ((dwi_in, dwi_out, 256), (dwo_in, dwo_out, 512)):
@@ -638,8 +664,11 @@
             d = pltpu.make_async_copy(src.at[here], dst.at[here], sem.at[len(moves)])
             d.start()
             moves.append(d)
-    mixed_ref[...] = dot(pick_ref[...], slots_ref[0], TN).astype(BF)
-    d_tok_ref[...] = dot(pick_ref[...], slots_ref[1], TN).astype(BF)
+    for t, out in enumerate((mixed_out, d_tok_out)):
+        spot[t] = dot(pick_ref[...], slots_ref[t], TN).astype(BF)
+        d = pltpu.make_async_copy(spot.at[t], out, sem.at[len(moves)])
+        d.start()
+        moves.append(d)
     for d in moves:
         d.wait()
 
@@ -657,8 +686,8 @@
             jax.ShapeDtypeStruct((2048, 1024), BF),
         ),
         in_specs=[vmem, vmem, anywhere, anywhere],
-        out_specs=(vmem, vmem, hbm, hbm),
-        scratch_shapes=[pltpu.SemaphoreType.DMA((8,))],
+        out_specs=(hbm, hbm, hbm, hbm),
+        scratch_shapes=[pltpu.VMEM((2, 256, 1024), BF), pltpu.SemaphoreType.DMA((10,))],
         compiler_params=pltpu.CompilerParams(vmem_limit_bytes=8 * 2**20),
         cost_estimate=pl.CostEstimate(
             flops=6 * 10**7, bytes_accessed=18 * 2**20, transcendentals=0

time: 91.5 us -> 93.3 us (1.020)
  Pallas kernels: 89.9 us -> 91.8 us
    pallas_call x1, Pallas kernels: 85.6 us -> 88.1 us  [exchange(): pl.pallas_call(kernel, out_shape=(pltpu.VMEM((64, 256), BF), pltpu.VMEM((...]
where the time goes in v5:
time: 93.3 us; the launch traced here: 93.2 us
  Pallas kernels  91.8 us (98%)
  between operations  1.45 us (2%)
    pallas_call x1, Pallas kernels, exchange(): pl.pallas_call(kernel, out_shape=(pltpu.VMEM((64, 256), BF), pltpu.VMEM((...  88.1 us
    pallas_call x1, Pallas kernels, finish(): pl.pallas_call(finish_kernel, out_shape=(jax.ShapeDtypeStruct((256, 1024)...  3.68 us

profile of v5, /device:TPU:0, one launch (start us, length us, event | category | flops | bytes accessed | tf_op | source)
XLA Modules:
  0.0 93.2 jit_solution(3182988350198003489)
XLA Ops:
  1.3 88.1 %shard_map.102 = (bf16[64,256]{1,0:T(8,128)(2,1)S(1)}, bf16[2,64,1024]{2,1,0:T(8,128)(2,1)S(1)}, bf16[1024,2048]{1,0:T(8,128)(2,1)S(1)}, bf16[2048,1024]{1,0:T(8,128)(2,1)S(1)}) custom-call(s32[1,64]{1,0:T(1,128)} %chosen_ref.1, f32[1,64]{1,0:T(1,128)} %gates_ref.1, s32[1,1]{1,0:T(1,128)} %bitcast.1.count_ref, bf16[256,1024]{1,0:T(8,128)(2,1)} %tok_hbm.1, ...), custom_call_target="tpu_custom_call" | custom-call | flops 14000000000 | bytes 20971520 | tf_op jit(solution)/shard_map/pallas_call | solution.py:609
  89.4 3.7 %shard_map.103 = (bf16[256,1024]{1,0:T(8,128)(2,1)}, bf16[256,1024]{1,0:T(8,128)(2,1)}, bf16[1024,2048]{1,0:T(8,128)(2,1)}, bf16[2048,1024]{1,0:T(8,128)(2,1)}) custom-call(bf16[64,256]{1,0:T(8,128)(2,1)S(1)} %get-tuple-element.8.pick_ref, bf16[2,64,1024]{2,1,0:T(8,128)(2,1)S(1)} %get-tuple-element.9.slots_ref, ...), custom_call_target="tpu_custom_call" | custom-call | flops 60000000 | bytes 18874368 | tf_op jit(solution)/shard_map/pallas_call | solution.py:680

commit v6 on v4

--- a/solution.py
+++ b/solution.py
@@ -425,9 +425,9 @@
             lax.fori_loop(0, 5, step, 0)
 
         def ct2():
+            sub[...] += product(c, wrap(y + 2))
             arrivals[-1][1]()
-            got = sub[...] + product(c, wrap(y + 2)) + product(oc, wrap(y + 2))
-            part[t, mine, :] = got.astype(BF)
+            part[t, mine, :] = (sub[...] + product(oc, wrap(y + 2))).astype(BF)
 
         if (t, half) == (1, 1):
             tasks["ct1_11"], tasks["ct2_11"] = ct1, ct2
@@ -629,7 +629,7 @@
 
 
 def finish_kernel(
-    pick_ref, slots_ref, dwi_in, dwo_in, mixed_ref, d_tok_ref, dwi_out, dwo_out, sem
+    pick_ref, slots_ref, dwi_in, dwo_in, mixed_out, d_tok_out, dwi_out, dwo_out, spot, sem
 ):
     moves = []
     for src, dst, n in ((dwi_in, dwi_out, 256), (dwo_in, dwo_out, 512)):
@@ -638,8 +638,11 @@
             d = pltpu.make_async_copy(src.at[here], dst.at[here], sem.at[len(moves)])
             d.start()
             moves.append(d)
-    mixed_ref[...] = dot(pick_ref[...], slots_ref[0], TN).astype(BF)
-    d_tok_ref[...] = dot(pick_ref[...], slots_ref[1], TN).astype(BF)
+    for t, out in enumerate((mixed_out, d_tok_out)):
+        spot[t] = dot(pick_ref[...], slots_ref[t], TN).astype(BF)
+        d = pltpu.make_async_copy(spot.at[t], out, sem.at[len(moves)])
+        d.start()
+        moves.append(d)
     for d in moves:
         d.wait()
 
@@ -657,8 +660,8 @@
             jax.ShapeDtypeStruct((2048, 1024), BF),
         ),
         in_specs=[vmem, vmem, anywhere, anywhere],
-        out_specs=(vmem, vmem, hbm, hbm),
-        scratch_shapes=[pltpu.SemaphoreType.DMA((8,))],
+        out_specs=(hbm, hbm, hbm, hbm),
+        scratch_shapes=[pltpu.VMEM((2, 256, 1024), BF), pltpu.SemaphoreType.DMA((10,))],
         compiler_params=pltpu.CompilerParams(vmem_limit_bytes=8 * 2**20),
         cost_estimate=pl.CostEstimate(
             flops=6 * 10**7, bytes_accessed=18 * 2**20, transcendentals=0

time: 91.5 us -> 91 us (level)
  no operation moved by 1% of the time
where the time goes in v6:
time: 91 us; the launch traced here: 90.9 us
  Pallas kernels  89.5 us (98%)
  between operations  1.45 us (2%)
    pallas_call x1, Pallas kernels, exchange(): pl.pallas_call(kernel, out_shape=(pltpu.VMEM((64, 256), BF), pltpu.VMEM((...  85.8 us
    pallas_call x1, Pallas kernels, finish(): pl.pallas_call(finish_kernel, out_shape=(jax.ShapeDtypeStruct((256, 1024)...  3.68 us

profile of v6, /device:TPU:0, one launch (start us, length us, event | category | flops | bytes accessed | tf_op | source)
XLA Modules:
  0.0 90.9 jit_solution(17310707144339735381)
XLA Ops:
  1.3 85.8 %shard_map.102 = (bf16[64,256]{1,0:T(8,128)(2,1)S(1)}, bf16[2,64,1024]{2,1,0:T(8,128)(2,1)S(1)}, bf16[1024,2048]{1,0:T(8,128)(2,1)S(1)}, bf16[2048,1024]{1,0:T(8,128)(2,1)S(1)}) custom-call(s32[1,64]{1,0:T(1,128)} %chosen_ref.1, f32[1,64]{1,0:T(1,128)} %gates_ref.1, s32[1,1]{1,0:T(1,128)} %bitcast.1.count_ref, bf16[256,1024]{1,0:T(8,128)(2,1)} %tok_hbm.1, ...), custom_call_target="tpu_custom_call" | custom-call | flops 14000000000 | bytes 20971520 | tf_op jit(solution)/shard_map/pallas_call | solution.py:584
  87.1 3.7 %shard_map.103 = (bf16[256,1024]{1,0:T(8,128)(2,1)}, bf16[256,1024]{1,0:T(8,128)(2,1)}, bf16[1024,2048]{1,0:T(8,128)(2,1)}, bf16[2048,1024]{1,0:T(8,128)(2,1)}) custom-call(bf16[64,256]{1,0:T(8,128)(2,1)S(1)} %get-tuple-element.8.pick_ref, bf16[2,64,1024]{2,1,0:T(8,128)(2,1)S(1)} %get-tuple-element.9.slots_ref, ...), custom_call_target="tpu_custom_call" | custom-call | flops 60000000 | bytes 18874368 | tf_op jit(solution)/shard_map/pallas_call | solution.py:654

commit v7 on v6

--- a/solution.py
+++ b/solution.py
@@ -19,19 +19,20 @@
 PHASES = ([(0, 1), (1, 1), (2, 1), (3, 1)], [(0, 2), (2, 2)])
 
 ORDER = (
-    "pick0", "ag1_00", "meta1", "ag1_01", "ag1_02", "ag1_03", "meta2", "ag2_01", "ag2_00", "meta",
-    "ag3_01", "buildct", "ag2_02", "ag2_03", "buildc0", "buildc1", "pick1", "ag1_10", "ag3_00",
-    "ag4_01", "ag4_00", "cmp_01", "ma_01", "cmp_00", "ma_00", "mb_01", "ag3_02", "mc_01", "mb_00",
-    "ag3_03", "mc_00", "md_01", "ag1_11", "md_00", "nb_01", "ag2_10", "ag4_02", "cmp_02", "ma_02",
-    "nb_00", "ag4_03", "cmp_03", "ma_03", "mb_02", "mc_02", "mb_03", "ag2_11", "fin_01", "md_02",
-    "mc_03", "fin_00", "nb_02", "ag3_10", "md_03", "nb_03", "fwd_00", "ag3_11", "fwd_01",
-    "ag4_10", "cmp_10", "fin_02", "ma_10", "fin_03", "mb_10", "ag4_11", "cmp_11", "ma_11",
-    "mc_10", "fwd_02", "opp_00", "mb_11", "mc_11", "opp_01", "fwd_03", "md_10", "nb_10", "md_11",
-    "opp_02", "ct_00", "opp_03", "nb_11", "ct_01", "fin_10", "e0_m", "dwo0", "e1_m", "fin_11",
-    "fn0_m", "fn1_m", "dwo1", "fwd_10", "fn2_m", "e2_m", "dwo2", "dwo3", "fwd_11", "fn3_m",
-    "fs0_m", "fs1_m", "opp_10", "ct1_11", "fs2_m", "opp_11", "ct_10", "ct2_11", "e0_d1", "e1_d1",
-    "dwo4", "dwi0", "fn0_d1", "fn1_d1", "fn2_d1", "dwo5", "dwi1", "e2_d1", "fn3_d1", "fs0_d1",
-    "fs3_m", "dwo6", "fs1_d1", "dwi2", "fs2_d1", "fs3_d1", "dwi3", "g3_m", "dwo7", "g3_d1",
+    "pick0", "ag1_00", "meta1", "pick1", "ag1_02", "ag1_03", "ag1_01", "meta2", "ag2_00",
+    "ag2_01", "ag2_02", "ag2_03", "meta", "buildc1", "buildc0", "ag3_00", "ag4_00", "cmp_00",
+    "ma_00", "ag3_01", "ag1_10", "mb_00", "mc_00", "ag3_02", "ag1_11", "md_00", "ag4_01",
+    "cmp_01", "ma_01", "ag3_03", "nb_00", "mb_01", "ag4_02", "cmp_02", "ma_02", "ag2_10", "mc_01",
+    "mb_02", "ag2_11", "ag4_03", "cmp_03", "md_01", "nb_01", "fin_00", "ma_03", "mc_02", "mb_03",
+    "ag3_10", "md_02", "nb_02", "mc_03", "fin_01", "ag3_11", "md_03", "nb_03", "fwd_00", "ag4_10",
+    "cmp_10", "ma_10", "fin_02", "mb_10", "ag4_11", "cmp_11", "fin_03", "ma_11", "mc_10",
+    "opp_00", "fwd_02", "fwd_01", "mb_11", "mc_11", "md_10", "fwd_03", "nb_10", "opp_02", "md_11",
+    "opp_01", "buildct", "nb_11", "opp_03", "ct_00", "fin_10", "ct_01", "fin_11", "e0_m", "e1_m",
+    "fwd_10", "dwo0", "dwo1", "e2_m", "fn0_m", "fn1_m", "fwd_11", "dwo2", "fn2_m", "fn3_m",
+    "opp_10", "ct1_11", "fs0_m", "opp_11", "ct_10", "fs1_m", "fs2_m", "ct2_11", "e0_d1", "dwi0",
+    "fs3_m", "e1_d1", "fn0_d1", "fn1_d1", "e2_d1", "fn2_d1", "fn3_d1", "dwo3", "dwi1", "dwo4",
+    "dwo5", "fs0_d1", "fs1_d1", "dwo6", "g3_m", "fs2_d1", "dwo7", "dwi2", "dwi3", "fs3_d1",
+    "g3_d1",
 )
 
 NN = (((1,), (0,)), ((), ()))

time: 91 us -> 90 us (0.989)
  Pallas kernels: 89.5 us -> 88.4 us
    pallas_call x1, Pallas kernels: 85.8 us -> 84.8 us  [exchange(): pl.pallas_call(kernel, out_shape=(pltpu.VMEM((64, 256), BF), pltpu.VMEM((...]
where the time goes in v7:
time: 90 us; the launch traced here: 89.9 us
  Pallas kernels  88.4 us (98%)
  between operations  1.45 us (2%)
    pallas_call x1, Pallas kernels, exchange(): pl.pallas_call(kernel, out_shape=(pltpu.VMEM((64, 256), BF), pltpu.VMEM((...  84.8 us
    pallas_call x1, Pallas kernels, finish(): pl.pallas_call(finish_kernel, out_shape=(jax.ShapeDtypeStruct((256, 1024)...  3.68 us

profile of v7, /device:TPU:0, one launch (start us, length us, event | category | flops | bytes accessed | tf_op | source)
XLA Modules:
  0.0 89.9 jit_solution(12295018206505204471)
XLA Ops:
  1.3 84.8 %shard_map.102 = (bf16[64,256]{1,0:T(8,128)(2,1)S(1)}, bf16[2,64,1024]{2,1,0:T(8,128)(2,1)S(1)}, bf16[1024,2048]{1,0:T(8,128)(2,1)S(1)}, bf16[2048,1024]{1,0:T(8,128)(2,1)S(1)}) custom-call(s32[1,64]{1,0:T(1,128)} %chosen_ref.1, f32[1,64]{1,0:T(1,128)} %gates_ref.1, s32[1,1]{1,0:T(1,128)} %bitcast.1.count_ref, bf16[256,1024]{1,0:T(8,128)(2,1)} %tok_hbm.1, ...), custom_call_target="tpu_custom_call" | custom-call | flops 14000000000 | bytes 20971520 | tf_op jit(solution)/shard_map/pallas_call | solution.py:585
  86.0 3.7 %shard_map.103 = (bf16[256,1024]{1,0:T(8,128)(2,1)}, bf16[256,1024]{1,0:T(8,128)(2,1)}, bf16[1024,2048]{1,0:T(8,128)(2,1)}, bf16[2048,1024]{1,0:T(8,128)(2,1)}) custom-call(bf16[64,256]{1,0:T(8,128)(2,1)S(1)} %get-tuple-element.8.pick_ref, bf16[2,64,1024]{2,1,0:T(8,128)(2,1)S(1)} %get-tuple-element.9.slots_ref, ...), custom_call_target="tpu_custom_call" | custom-call | flops 60000000 | bytes 18874368 | tf_op jit(solution)/shard_map/pallas_call | solution.py:655
